TPU v7x, 32 devices: a whole 2x2x4 slice. The times are simulated.
32 devices in a mesh: tm: 4 (over y, core), chan: 8 (over z, x).
Axes of the slice: x: 2, y: 2, z: 4, core: 2. Of those that a mesh axis runs over, the one named last changes fastest.
Arguments:
- filterbank: bfloat16 [1024, 1024], P('chan', 'tm'), may hold values from -6 to 6
- chan_delay: int32 [1024], replicated, may hold values from 0 to 4096, as said below
- tail_len: int32 [32], replicated, may hold values from 1 to 256, as said below
- kernels: bfloat16 [2, 32, 256], replicated, may hold values from -0.375 to 0.375
Outputs:
- accel_power: bfloat16 [32, 32, 512], P(None, 'chan', 'tm')
Inputs may be any that keep to these rules, and one draw needn't show every extreme that they name: `chan_delay`: some channel has exactly 4096. `tail_len`: some trial has exactly 256.
All inputs are finite; a program needn't handle non-finite values.
Results may differ from a plain program's by a relative error of at most 0.011.
Values may be sent and summed in bfloat16 or wider, within the bound.
No kernel may reach another device: no remote copies, remote signals or barrier semaphores. Data moves between devices by JAX's collectives and lax.ppermute only.
A program may use at most 64 MiB of HBM per device.

v0:
```python
import math

import jax
import jax.numpy as jnp
from jax import lax
from jax.sharding import PartitionSpec as P

CHANNELS = 1024
TRIAL_DEV = 4
MAXDELAY = 4096


def from_behind(value, axis, steps):
    count = lax.axis_size(axis)
    leading, last = (max(0, -steps), min(count, count - steps))
    return lax.ppermute(value, axis, [(source, source + steps) for source in range(leading, last)])


def forward_table(block_len):
    period = 2 * block_len
    sample_idx = jnp.arange(block_len, dtype=jnp.int32)
    phases = sample_idx[:, None] * sample_idx[None, :] % period
    angles = phases.astype(jnp.float32) * (2.0 * math.pi / period)
    return jnp.concatenate([jnp.cos(angles), -jnp.sin(angles)], axis=1).astype(jnp.bfloat16)


def inverse_table(block_len):
    period = 2 * block_len
    bin_index = jnp.arange(block_len, dtype=jnp.int32)
    position = jnp.arange(period, dtype=jnp.int32)
    offsets = (position + block_len) % period
    phases = bin_index[:, None] * offsets[None, :] % period
    angles = phases.astype(jnp.float32) * (2.0 * math.pi / period)
    weights = jnp.where(bin_index == 0, 1.0, 2.0).astype(jnp.bfloat16)[:, None]
    cosines = jnp.cos(angles).astype(jnp.bfloat16)
    sine_vals = jnp.sin(angles).astype(jnp.bfloat16)
    return jnp.concatenate([cosines * weights, -(sine_vals * weights)], axis=0)


def block_table(block_len):
    half_len = block_len // 2
    sample_idx = jnp.arange(block_len, dtype=jnp.int32)
    bin_index = jnp.arange(half_len, dtype=jnp.int32)
    phases = sample_idx[:, None] * bin_index[None, :] % block_len
    angles = phases.astype(jnp.float32) * (2.0 * math.pi / block_len)
    return jnp.concatenate([jnp.cos(angles), -jnp.sin(angles)], axis=1).astype(jnp.bfloat16)


def kernel_weights(kernels):
    real_kernel = kernels[0]
    imag_kernel = kernels[1]
    upper_rows = jnp.stack([real_kernel, -imag_kernel], axis=1)
    lower_rows = jnp.stack([imag_kernel, real_kernel], axis=1)
    return jnp.concatenate([upper_rows, lower_rows], axis=0)


def spectrum_of(samples, forward):
    block_len = samples.shape[1]
    spectra = jnp.dot(samples, forward, preferred_element_type=jnp.float32) * (
        1.0 / math.sqrt(block_len)
    )
    return spectra.astype(jnp.bfloat16).reshape(samples.shape[0], 2, block_len)


def dedisperse(spectra, delays, tail_sizes):
    row_count = spectra.shape[0]
    trial_count = tail_sizes.shape[0]
    bin_count = spectra.shape[2]
    period = 2 * bin_count
    bin_span = min(bin_count, 128)
    block_count = bin_count // bin_span
    shifts = tail_sizes[:, None] * delays[None, :] // MAXDELAY
    blocks = spectra.reshape(row_count, 2, block_count, bin_span).transpose(2, 0, 1, 3)
    angle_step = 2.0 * math.pi / period

    def bin_block(unused, scan_item):
        block_index, spectra_part = scan_item
        bin_index = block_index * bin_span + lax.iota(jnp.int32, bin_span)
        phases = shifts[:, :, None] * bin_index[None, None, :] % period
        angles = phases.astype(jnp.float32) * angle_step
        ramp_cos = lax.optimization_barrier(jnp.cos(angles).astype(jnp.bfloat16)).astype(
            jnp.float32
        )
        ramp_sin = lax.optimization_barrier(jnp.sin(angles).astype(jnp.bfloat16)).astype(
            jnp.float32
        )
        real_part = spectra_part[:, 0].astype(jnp.float32)[None]
        imag_part = spectra_part[:, 1].astype(jnp.float32)[None]
        out_real = jnp.sum(real_part * ramp_cos - imag_part * ramp_sin, axis=1)
        out_imag = jnp.sum(real_part * ramp_sin + imag_part * ramp_cos, axis=1)
        return (unused, jnp.stack([out_real, out_imag], axis=0))

    block_ids = jnp.arange(block_count, dtype=jnp.int32)
    unused, stacked = lax.scan(bin_block, jnp.zeros((), jnp.float32), (block_ids, blocks))
    return stacked.transpose(2, 1, 0, 3).reshape(trial_count, 2, bin_count) * (
        1.0 / math.sqrt(CHANNELS)
    )


def shards(filterbank, chan_delay, tail_len, kernels):
    block_len = filterbank.shape[1]
    half_len = block_len // 2
    forward = forward_table(block_len)
    first_trial = lax.axis_index("chan") * TRIAL_DEV
    own_tails = lax.dynamic_slice_in_dim(tail_len, first_trial, TRIAL_DEV)
    own_spectra = spectrum_of(filterbank, forward)
    dedispersed = dedisperse(
        lax.all_gather(own_spectra, "chan", axis=0, tiled=True), chan_delay, own_tails
    )
    rounded = dedispersed.astype(jnp.bfloat16).reshape(TRIAL_DEV, 2 * block_len)
    inverse = inverse_table(block_len)
    out_scale = 0.5 / math.sqrt(block_len)
    full_series = jnp.dot(rounded, inverse, preferred_element_type=jnp.float32) * out_scale
    tail_early = full_series[:, :block_len]
    positions = lax.iota(jnp.int32, block_len)
    keep_mask = positions[None, :] >= block_len - own_tails[:, None]
    tail_parts = jnp.where(keep_mask, tail_early, 0.0)
    received = from_behind(tail_parts, "tm", -1)
    body_late = full_series[:, block_len:]
    series = (body_late + received).astype(jnp.bfloat16)
    blocked = block_table(block_len)
    spectra_blocks = (
        jnp.dot(series, blocked, preferred_element_type=jnp.float32) * (1.0 / math.sqrt(block_len))
    ).astype(jnp.bfloat16)
    spectra_blocks = spectra_blocks.reshape(TRIAL_DEV, 2, half_len)
    weights = kernel_weights(kernels)
    tap_count = kernels.shape[2]
    correlation = lax.conv_general_dilated(
        spectra_blocks,
        weights,
        (1,),
        [(tap_count // 2, tap_count - 1 - tap_count // 2)],
        preferred_element_type=jnp.float32,
    )
    accel_count = kernels.shape[1]
    power_out = (
        correlation[:, :accel_count] * correlation[:, :accel_count]
        + correlation[:, accel_count:] * correlation[:, accel_count:]
    )
    return power_out.transpose(1, 0, 2).astype(jnp.bfloat16)


def solution(mesh):
    placed = (P("chan", "tm"), P(), P(), P())
    return jax.shard_map(
        shards, mesh=mesh, in_specs=placed, out_specs=P(None, "chan", "tm"), check_vma=False
    )
```

profile of v0, /device:TPU:0, one launch (start us, length us, event | category | flops | bytes accessed | tf_op | source)
XLA Modules:
  0.0 91.3 jit_solution(3698861419978128044)
XLA Ops:
  6.5 0.0 copy-start
  6.5 0.0 copy-start.2
  6.5 0.0 copy-start.1
  6.5 0.0 all-gather.2.cloned.1.call-start
  6.5 1.1 %negate_convert_fusion = (bf16[256,256]{1,0:T(8,128)(2,1)S(1)}, bf16[256,256]{1,0:T(8,128)(2,1)S(1)}) fusion(), kind=kLoop, calls=%fused_computation.68 | loop fusion | flops 1114112 | bytes 262144 | tf_op jit(solution)/shard_map/convert.5
  7.7 0.0 copy-done
  7.7 0.9 fusion.15
  8.6 0.0 all-gather.2.cloned.1.call-update
  8.6 0.7 broadcast_subtract_fusion
  9.4 0.5 negate_convert_fusion.1
  9.9 0.0 copy-done.2
  10.0 2.2 %fusion.29 = (bf16[256,512]{1,0:T(8,128)(2,1)S(1)}, bf16[256,512]{1,0:T(8,128)(2,1)S(1)}) fusion(s32[512]{0:T(512)S(1)} %add_select_fusion.5, bf16[256]{0:T(256)(128)(2,1)S(1)} %fusion.52), kind=kLoop, calls=%fused_computation.62 | loop fusion | flops 3145728 | bytes 526848 | tf_op jit(solution)/shard_map/mul | solution.py:37
  12.2 39.5 %all-gather.2.cloned.1.call-done = bf16[1024,2,256]{0,2,1:T(8,128)(2,1)} async-done(((bf16[128,2,256]{0,2,1:T(8,128)(2,1)}), bf16[1024,2,256]{0,2,1:T(8,128)(2,1)}) %all-gather.2.cloned.1.call-update) | async-done | bytes 1048592 | tf_op jit(solution)/shard_map/all_gather | solution.py:108
  51.7 0.0 copy-done.1
  51.7 24.9 %while.13 = (s32[]{:T(128)}, f32[2,2,4,128]{3,2,1,0:T(4,128)S(1)}, bf16[2,1024,2,128]{1,3,0,2:T(8,128)(2,1)}, s32[2]{0:T(128)S(1)}, s32[1024]{0:T(1024)S(1)}, /*index=5*/s32[4]{0:T(128)S(1)}, s32[]{:T(128)}, s32[1]{0:T(128)}) while((s32[]{:T(128)}, f32[2,2,4,128]{3,2,1,0:T(4,128)S(1)}, bf16[2,1024,2,128]{1,3,0,2:T(8,128)(2,1)}, ...), condition=%wide.region_3.4_spmd.clone, body=%wide.region_0.3_spmd.clone.sunk | while | flops 13959299 | bytes 8963217 | solution.py:94
  51.7 0.6 dynamic_slice.25
  52.8 0.1 add_select_fusion.7
  52.9 1.1 %constant_dynamic-slice_fusion.2 = bf16[1,1024,2,128]{1,3,0,2:T(8,128)(2,1)S(1)} fusion(bf16[2,1024,2,128]{1,3,0,2:T(8,128)(2,1)} %get-tuple-element.203, s32[]{:T(128)S(6)} %copy.33), kind=kLoop, calls=%fused_computation.36.clone.1 | loop fusion | bytes 1048580 | tf_op jit(solution)/shard_map/while/body/jit(dynamic_index_in_dim)/dynamic_slice | solution.py:94
  54.0 0.3 copy.29
  54.3 0.1 fusion.66
  54.4 9.0 %sine_convert_fusion.3 = (bf16[4,1024,128]{2,1,0:T(8,128)(2,1)S(1)}, bf16[4,1024,128]{2,1,0:T(8,128)(2,1)S(1)}) fusion(s32[128]{0:T(128)S(1)} %iota_add_fusion.2, s32[4,1024]{1,0:T(4,128)S(1)} %add_select_fusion.7), kind=kLoop, calls=%fused_computation.17.clone.1 | loop fusion | flops 8388608 | bytes 2114048 | tf_op jit(solution)/shard_map/while/body/eval_jaxpr/convert_element_type | solution.py:84
  63.4 0.7 fusion.67
  64.1 0.6 dynamic_slice.25
  65.3 0.1 add_select_fusion.7
  65.4 1.1 %constant_dynamic-slice_fusion.2 = bf16[1,1024,2,128]{1,3,0,2:T(8,128)(2,1)S(1)} fusion(bf16[2,1024,2,128]{1,3,0,2:T(8,128)(2,1)} %get-tuple-element.203, s32[]{:T(128)S(6)} %copy.33), kind=kLoop, calls=%fused_computation.36.clone.1 | loop fusion | bytes 1048580 | tf_op jit(solution)/shard_map/while/body/jit(dynamic_index_in_dim)/dynamic_slice | solution.py:94
  66.5 0.3 copy.29
  66.7 0.1 fusion.66
  66.8 9.0 %sine_convert_fusion.3 = (bf16[4,1024,128]{2,1,0:T(8,128)(2,1)S(1)}, bf16[4,1024,128]{2,1,0:T(8,128)(2,1)S(1)}) fusion(s32[128]{0:T(128)S(1)} %iota_add_fusion.2, s32[4,1024]{1,0:T(4,128)S(1)} %add_select_fusion.7), kind=kLoop, calls=%fused_computation.17.clone.1 | loop fusion | flops 8388608 | bytes 2114048 | tf_op jit(solution)/shard_map/while/body/eval_jaxpr/convert_element_type | solution.py:84
  75.8 0.7 fusion.67
  76.6 0.2 convolution_multiply_fusion.1
  76.7 0.1 slice_select_fusion
  76.8 1.3 %collective-permute-start = (f32[4,256]{1,0:T(4,128)S(1)}, f32[4,256]{1,0:T(4,128)S(1)}, u32[]{:S(2)}, u32[]{:S(2)}) collective-permute-start(f32[4,256]{1,0:T(4,128)S(1)} %slice_select_fusion), channel_id=1, source_target_pairs={{8,0},{16,8},{24,16},{9,1},{17,9},{25,17},{10,2},{18,10},{26,18},{... | collective-permute-start | bytes 12296 | tf_op jit(solution)/shard_map/ppermute | solution.py:16
  78.1 0.2 reverse.3
  78.4 0.1 copy.20
  78.5 1.4 %collective-permute-done = f32[4,256]{1,0:T(4,128)S(1)} collective-permute-done((f32[4,256]{1,0:T(4,128)S(1)}, f32[4,256]{1,0:T(4,128)S(1)}, u32[]{:S(2)}, u32[]{:S(2)}) %collective-permute-start) | collective-permute-done | bytes 4128 | tf_op jit(solution)/shard_map/ppermute | solution.py:16
  79.9 0.1 fusion.16
  80.0 0.2 copy.21
  80.2 3.2 %fusion.58 = f32[4,64,128]{1,0,2:T(4,128)S(1)} fusion(bf16[64,2,256]{0,1,2:T(2,128)(2,1)S(1)} %copy.20, bf16[4,2,128]{0,1,2:T(2,128)(2,1)S(1)} %copy.21), kind=kOutput, calls=%fused_computation.110 | convolution fusion | flops 16777216 | bytes 198656 | tf_op jit(solution)/shard_map/conv_general_dilated | solution.py:128
  83.4 0.2 fusion.57
  83.6 0.1 copy.26
  83.7 0.1 copy.27
  83.9 0.6 copy.24
  (15 shorter events, 0.1 us)
Async XLA Ops:
  6.5 1.1 %copy-start = (bf16[128,256]{1,0:T(8,128)(2,1)S(1)}, bf16[128,256]{1,0:T(8,128)(2,1)}, u32[]{:S(2)}) copy-start(bf16[128,256]{1,0:T(8,128)(2,1)} %param.6) | copy-start | bytes 196612
  6.5 3.4 %copy-start.2 = (bf16[2,32,256]{2,1,0:T(8,128)(2,1)S(1)}, bf16[2,32,256]{2,1,0:T(8,128)(2,1)}, u32[]{:S(2)}) copy-start(bf16[2,32,256]{2,1,0:T(8,128)(2,1)} %param.9) | copy-start | bytes 98308
  6.5 45.1 %copy-start.1 = (s32[1024]{0:T(1024)S(1)}, s32[1024]{0:T(1024)}, u32[]{:S(2)}) copy-start(s32[1024]{0:T(1024)} %param.7) | copy-start | bytes 12292
  6.5 45.1 %all-gather.2.cloned.1.call-start = ((), (), s32[]{:S(2)}) async-start(), calls=%async_computation | async-start | bytes 1179648 | tf_op jit(solution)/shard_map/all_gather | solution.py:108
  76.8 3.1 %collective-permute-start = (f32[4,256]{1,0:T(4,128)S(1)}, f32[4,256]{1,0:T(4,128)S(1)}, u32[]{:S(2)}, u32[]{:S(2)}) collective-permute-start(f32[4,256]{1,0:T(4,128)S(1)} %slice_select_fusion), channel_id=1, source_target_pairs={{8,0},{16,8},{24,16},{9,1},{17,9},{25,17},{10,2},{18,10},{26,18},{... | collective-permute-start | bytes 12296 | tf_op jit(solution)/shard_map/ppermute | solution.py:16
Sparse Core Ops, SparseCore 0:
  9.4 42.2 all-gather.1
where the time goes:
time: 92.9 us; the launch traced here: 91.3 us
  waiting for transfers between devices  40.9 us (44%)
  other arithmetic  24.5 us (26%)
  between operations  13.5 us (15%)
  local copies, waits for them, and re-layouts  5.46 us (6%)
  matrix products  4.42 us (5%)
  starting transfers between devices  1.3 us (1%)
  loops' own time  1.25 us (1%)
    all_gather x1, waiting for transfers between devices, shards(): lax.all_gather(own_spectra, 'chan', axis=0, tiled=True)  39.5 us
    convert_element_type x2, other arithmetic, bin_block(): jnp.sin(angles).astype(jnp.bfloat16)  18 us
    dynamic_slice x6, local copies, waits for them, and re-layouts, dedisperse(): lax.scan(bin_block, jnp.zeros((), jnp.float32), (block_ids, blocks))  3.86 us
    conv_general_dilated x1, matrix products, shards(): lax.conv_general_dilated(spectra_blocks, weights, (1,), [(tap_count // 2,...  3.2 us
    mul x1, other arithmetic, inverse_table(): return jnp.concatenate([cosines * weights, -(sine_vals * weights)], axis=0)  2.25 us
  transfers between devices with their start and end apart: 2, of which 2 were waited for; matrix products, arithmetic and copies ran while one was open for 4% of the time, Pallas kernels for 0%

commit v1 on v0

v1 whole, which is shorter than its diff:
```python
import functools
import math

import jax
import jax.numpy as jnp
import numpy as np
from jax import lax
from jax.experimental import pallas as pl
from jax.experimental.pallas import tpu as pltpu
from jax.sharding import PartitionSpec as P

TRIAL_DEV = 4
MAXDELAY = 4096
LANES = 128
FINE = 16
COARSE = LANES // FINE
ROWS = 2 * TRIAL_DEV


def bin_table(block_len):
    half_len = block_len // 2
    samples = np.arange(half_len)
    angles = (samples[:, None] * samples[None, :] % block_len) * (2.0 * math.pi / block_len)
    table = np.concatenate([np.cos(angles), -np.sin(angles)], axis=1)
    return jnp.asarray(table.astype(np.float32), jnp.bfloat16)


def shift_left(value, steps):
    width = value.shape[1]
    return pltpu.roll(value, width - steps, 1)


def as_column(row):
    count = row.shape[1]
    rows = lax.broadcasted_iota(jnp.int32, (count, count), 0)
    columns = lax.broadcasted_iota(jnp.int32, (count, count), 1)
    return jnp.sum(jnp.where(rows == columns, row, 0), axis=1, keepdims=True)


def trial_blocks(value, chan_count):
    parts = []
    for owner in range(chan_count):
        rows = value[owner * TRIAL_DEV : (owner + 1) * TRIAL_DEV]
        parts += [rows[:, :LANES], rows[:, LANES:]]
    return jnp.concatenate(parts, axis=0).astype(jnp.bfloat16)


def partial_series(tm_count, chan_count, samples_ref, delay_ref, tail_ref, out_ref, moved, chosen):
    channels, block_len = samples_ref.shape
    trials = tail_ref.shape[1]
    samples = samples_ref[...]
    padded = jnp.concatenate([jnp.zeros((channels, LANES), jnp.bfloat16), samples], axis=1)
    for coarse in range(COARSE):
        moved[coarse * channels : (coarse + 1) * channels, :] = (
            shift_left(padded, FINE * coarse) if coarse else padded
        )

    delays = delay_ref[pl.ds(lax.axis_index("chan"), 1), :]
    tails = as_column(tail_ref[...])
    shifts = lax.shift_right_logical(delays * tails, MAXDELAY.bit_length() - 1)
    shift_vals = shifts.astype(jnp.float32)
    rests = jnp.concatenate([shift_vals - FINE * coarse for coarse in range(COARSE)], axis=1)
    rests = rests.astype(jnp.bfloat16)
    one = jnp.ones((), jnp.bfloat16)
    zero = jnp.zeros((), jnp.bfloat16)
    for part in range(2):
        for fine in range(FINE):
            first = (part * FINE + fine) * trials
            wanted = jnp.array(part * LANES + fine, jnp.bfloat16)
            chosen[first : first + trials, :] = jnp.where(rests == wanted, one, zero)
    sums = jnp.dot(chosen[...], moved[...], preferred_element_type=jnp.float32)

    level = []
    for fine in range(FINE):
        near = sums[fine * trials : (fine + 1) * trials]
        far = sums[(FINE + fine) * trials : (FINE + fine + 1) * trials]
        level.append(
            jnp.concatenate(
                [
                    far[:, :LANES],
                    far[:, LANES : 2 * LANES] + near[:, :LANES],
                    far[:, 2 * LANES :] + near[:, LANES : 2 * LANES],
                    near[:, 2 * LANES :],
                ],
                axis=1,
            )
        )
    steps = 1
    while len(level) > 1:
        level = [
            level[2 * i] + shift_left(level[2 * i + 1], steps) for i in range(len(level) // 2)
        ]
        steps *= 2
    series = level[0]

    rows = lax.broadcasted_iota(jnp.int32, (block_len, LANES), 0)
    columns = lax.broadcasted_iota(jnp.int32, (block_len, LANES), 1)
    nyquist_step = 0.5 / block_len
    alternating = jnp.where((rows + columns) % 2 == 0, -nyquist_step, nyquist_step)
    nyquist = jnp.dot(samples, alternating.astype(jnp.bfloat16), preferred_element_type=jnp.float32)
    parity = jnp.where(shifts % 2 == 0, 1.0, -1.0).astype(jnp.bfloat16)
    top_bin = jnp.dot(parity, nyquist.astype(jnp.bfloat16), preferred_element_type=jnp.float32)
    top_bin = jnp.concatenate([top_bin, top_bin], axis=1)
    whole = jnp.where(shifts == block_len, 1.0, 0.0).astype(jnp.bfloat16)
    whole_block = jnp.dot(whole, samples, preferred_element_type=jnp.float32)

    scale = 1.0 / math.sqrt(channels * chan_count)
    late = (series[:, block_len:] + top_bin) * scale
    early = (series[:, :block_len] + top_bin + whole_block) * scale
    positions = lax.broadcasted_iota(jnp.int32, (trials, block_len), 1)
    early = jnp.where(positions >= block_len - tails, early, 0.0)

    group_rows = chan_count * ROWS
    group = lax.axis_index("tm")
    out_ref[...] = jnp.zeros_like(out_ref)
    out_ref[pl.ds(pl.multiple_of(group * group_rows, group_rows), group_rows), :] = trial_blocks(
        late, chan_count
    )

    @pl.when(group > 0)
    def _():
        before = pl.multiple_of((group - 1) * group_rows, group_rows)
        out_ref[pl.ds(before, group_rows), :] = trial_blocks(early, chan_count)


def accel_search(tm_count, chan_count, parts_ref, table_ref, kernels_ref, out_ref):
    group_rows = chan_count * ROWS
    group = lax.axis_index("tm")
    after = lax.rem(group + 1, tm_count)
    own = parts_ref[pl.ds(pl.multiple_of(group * group_rows, group_rows), group_rows), :]
    following = parts_ref[pl.ds(pl.multiple_of(after * group_rows, group_rows), group_rows), :]
    both = own.astype(jnp.float32) + following.astype(jnp.float32)
    series = jnp.sum(both.reshape(chan_count, ROWS, LANES), axis=0).astype(jnp.bfloat16)

    half_len = LANES
    block_len = 2 * half_len
    halves = jnp.dot(series, table_ref[...], preferred_element_type=jnp.float32)
    columns = lax.broadcasted_iota(jnp.int32, (TRIAL_DEV, block_len), 1)
    signs = jnp.where(columns % 2 == 0, 1.0, -1.0)
    spectra = (halves[:TRIAL_DEV] + signs * halves[TRIAL_DEV:]) * (1.0 / math.sqrt(block_len))
    spectra = spectra.astype(jnp.bfloat16).astype(jnp.float32)

    sublanes = lax.broadcasted_iota(jnp.int32, (8, block_len), 0)
    zeros = jnp.zeros((8, half_len), jnp.float32)
    taps = []
    for trial in range(TRIAL_DEV):
        windows = []
        for first in (0, half_len):
            row = spectra[trial : trial + 1, first : first + half_len]
            wide = jnp.concatenate([zeros, jnp.broadcast_to(row, (8, half_len))], axis=1)
            for steps in (1, 2, 4):
                wide = jnp.where(sublanes & steps != 0, shift_left(wide, steps), wide)
            for start in range(0, block_len, 8):
                windows.append((shift_left(wide, start) if start else wide)[:, :half_len])
        taps.append(jnp.concatenate(windows, axis=0).astype(jnp.bfloat16))
    windows = jnp.concatenate(taps, axis=1)

    real = kernels_ref[0]
    imag = kernels_ref[1]
    weights = jnp.concatenate(
        [jnp.concatenate([real, -imag], axis=1), jnp.concatenate([imag, real], axis=1)], axis=0
    )
    correlation = jnp.dot(weights, windows, preferred_element_type=jnp.float32)
    accels = real.shape[0]
    power = correlation[:accels] * correlation[:accels] + correlation[accels:] * correlation[accels:]
    for trial in range(TRIAL_DEV):
        out_ref[:, trial, :] = power[:, trial * half_len : (trial + 1) * half_len].astype(
            jnp.bfloat16
        )


def shards(tm_count, chan_count, filterbank, chan_delay, tail_len, kernels):
    channels, block_len = filterbank.shape
    trials = tail_len.shape[0]
    accels = kernels.shape[1]
    devices = tm_count * chan_count
    parts = pl.pallas_call(
        functools.partial(partial_series, tm_count, chan_count),
        out_shape=jax.ShapeDtypeStruct((devices * ROWS, LANES), jnp.bfloat16),
        scratch_shapes=[
            pltpu.VMEM((COARSE * channels, block_len + LANES), jnp.bfloat16),
            pltpu.VMEM((2 * FINE * trials, COARSE * channels), jnp.bfloat16),
        ],
        compiler_params=pltpu.CompilerParams(vmem_limit_bytes=40 * 1024 * 1024),
        name="partial_series",
    )(filterbank, chan_delay.reshape(chan_count, channels), tail_len.reshape(1, trials))
    parts = lax.all_to_all(parts, ("tm", "chan"), 0, 0, tiled=True)
    return pl.pallas_call(
        functools.partial(accel_search, tm_count, chan_count),
        out_shape=jax.ShapeDtypeStruct((accels, TRIAL_DEV, block_len // 2), jnp.bfloat16),
        compiler_params=pltpu.CompilerParams(vmem_limit_bytes=40 * 1024 * 1024),
        name="accel_search",
    )(parts, bin_table(block_len), kernels)


def solution(mesh):
    placed = (P("chan", "tm"), P(), P(), P())
    return jax.shard_map(
        functools.partial(shards, mesh.shape["tm"], mesh.shape["chan"]),
        mesh=mesh,
        in_specs=placed,
        out_specs=P(None, "chan", "tm"),
        check_vma=False,
    )
```

time: 92.9 us -> 20 us (0.22); the launches traced: 91.3 us -> 19.8 us
  waiting for transfers between devices: 40.9 us -> 0 us
  other arithmetic: 24.5 us -> 0 us
  blocking collectives: 0 us -> 14.4 us
  between operations: 13.5 us -> 0.03 us
  matrix products: 4.42 us -> 0 us
  local copies, waits for them, and re-layouts: 5.46 us -> 2.19 us
  Pallas kernels: 0 us -> 3.19 us
  starting transfers between devices: 1.3 us -> 0 us
  loops' own time: 1.25 us -> 0 us
    all_gather x1 -> x0, waiting for transfers between devices: 39.5 us -> none  [shards(): lax.all_gather(own_spectra, 'chan', axis=0, tiled=True)]
    convert_element_type x7 -> x0, other arithmetic: 18.2 us -> none  [the longest x2 18 us: bin_block(): jnp.sin(angles).astype(jnp.bfloat16)]
    all_to_all x0 -> x1, blocking collectives: none -> 14.4 us  [shards(): parts = lax.all_to_all(parts, ('tm', 'chan'), 0, 0, tiled=True)]
    dynamic_slice x6 -> x0, local copies, waits for them, and re-layouts: 3.86 us -> none  [dedisperse(): lax.scan(bin_block, jnp.zeros((), jnp.float32), (block_ids, blocks))]
    conv_general_dilated x1 -> x0, matrix products: 3.2 us -> none  [shards(): lax.conv_general_dilated(spectra_blocks, weights, (1,), [(tap_count // 2,...]
    pallas_call x0 -> x2, Pallas kernels: none -> 3.19 us  [the longest x1 1.75 us: shards(): pl.pallas_call(functools.partial(partial_series, tm_count, chan_count), o...]
    mul x1 -> x0, other arithmetic: 2.25 us -> none  [inverse_table(): return jnp.concatenate([cosines * weights, -(sine_vals * weights)], axis=0)]
    unnamed x8 -> x10, local copies, waits for them, and re-layouts: 0.23 us -> 2.19 us
  transfers between devices with their start and end apart: 2 -> 0, of which waited for: 2 -> 0; matrix products, arithmetic and copies ran while one was open for 4% -> 0% of each run, Pallas kernels for 0% -> 0%
where the time goes in v1:
time: 20 us; the launch traced here: 19.8 us
  blocking collectives  14.4 us (72%)
  Pallas kernels  3.19 us (16%)
  local copies, waits for them, and re-layouts  2.19 us (11%)
    all_to_all x1, blocking collectives, shards(): parts = lax.all_to_all(parts, ('tm', 'chan'), 0, 0, tiled=True)  14.4 us
    unnamed x10, local copies, waits for them, and re-layouts  2.19 us
    pallas_call x1, Pallas kernels, shards(): pl.pallas_call(functools.partial(partial_series, tm_count, chan_count), o...  1.75 us
    pallas_call x1, Pallas kernels, shards(): pl.pallas_call(functools.partial(accel_search, tm_count, chan_count), out...  1.44 us

profile of v1, /device:TPU:0, one launch (start us, length us, event | category | flops | bytes accessed | tf_op | source)
XLA Modules:
  0.0 19.8 jit_solution(3267688633108732736)
XLA Ops:
  0.0 0.0 copy-start.4
  0.0 0.7 %copy-done.4 = s32[32]{0:T(128)S(1)} copy-done((s32[32]{0:T(128)S(1)}, s32[32]{0:T(128)}, u32[]{:S(2)}) %copy-start.4) | copy-done | bytes 152
  0.7 0.0 copy-start.1
  0.7 0.8 %copy-done.1 = bf16[128,256]{1,0:T(8,128)(2,1)S(1)} copy-done((bf16[128,256]{1,0:T(8,128)(2,1)S(1)}, bf16[128,256]{1,0:T(8,128)(2,1)}, u32[]{:S(2)}) %copy-start.1) | copy-done | bytes 65560
  1.5 0.0 copy-start.3
  1.5 0.7 %copy-done.3 = s32[1024]{0:T(1024)S(1)} copy-done((s32[1024]{0:T(1024)S(1)}, s32[1024]{0:T(1024)}, u32[]{:S(2)}) %copy-start.3) | copy-done | bytes 4120
  2.2 1.8 %partial_series.1 = bf16[256,128]{1,0:T(8,128)(2,1)S(1)} custom-call(bf16[128,256]{1,0:T(8,128)(2,1)S(1)} %copy-done.1, s32[8,128]{1,0:T(8,128)S(1)} %bitcast.6, s32[1,32]{1,0:T(1,128)S(1)} %bitcast.7), custom_call_target="tpu_custom_call" | custom-call | tf_op jit(solution)/shard_map/partial_series/pallas_call | solution.py:177
  3.9 0.0 copy-start
  4.0 0.0 copy-start.2
  4.0 14.4 %all_to_all.11 = bf16[32,8,128]{2,1,0:T(8,128)(2,1)S(1)} all-to-all(bf16[32,8,128]{2,1,0:T(8,128)(2,1)S(1)} %bitcast.5), channel_id=1, replica_groups=mesh['tm'=4,'chan'=8] {'tm','chan'}, dimensions={0} | all-to-all | bytes 131072 | tf_op jit(solution)/shard_map/all_to_all | solution.py:187
  18.3 0.0 copy-done
  18.3 0.0 copy-done.2
  18.4 1.4 %accel_search.1 = bf16[32,4,128]{2,1,0:T(4,128)(2,1)} custom-call(bf16[256,128]{1,0:T(8,128)(2,1)S(1)} %bitcast.4, bf16[128,256]{1,0:T(8,128)(2,1)S(1)} %copy-done, bf16[2,32,256]{2,1,0:T(8,128)(2,1)S(1)} %copy-done.2), custom_call_target="tpu_custom_call" | custom-call | tf_op jit(solution)/shard_map/accel_search/pallas_call | solution.py:188
Async XLA Ops:
  0.0 0.7 %copy-start.4 = (s32[32]{0:T(128)S(1)}, s32[32]{0:T(128)}, u32[]{:S(2)}) copy-start(s32[32]{0:T(128)} %param.7) | copy-start | bytes 388
  0.7 0.8 %copy-start.1 = (bf16[128,256]{1,0:T(8,128)(2,1)S(1)}, bf16[128,256]{1,0:T(8,128)(2,1)}, u32[]{:S(2)}) copy-start(bf16[128,256]{1,0:T(8,128)(2,1)} %samples_ref.1) | copy-start | bytes 196612
  1.5 0.7 %copy-start.3 = (s32[1024]{0:T(1024)S(1)}, s32[1024]{0:T(1024)}, u32[]{:S(2)}) copy-start(s32[1024]{0:T(1024)} %param.6) | copy-start | bytes 12292
  3.9 14.4 %copy-start = (bf16[128,256]{1,0:T(8,128)(2,1)S(1)}, bf16[128,256]{1,0:T(8,128)(2,1)}, u32[]{:S(2)}) copy-start(bf16[128,256]{1,0:T(8,128)(2,1)} %constant.2.clone.table_ref) | copy-start | bytes 196612
  4.0 14.4 %copy-start.2 = (bf16[2,32,256]{2,1,0:T(8,128)(2,1)S(1)}, bf16[2,32,256]{2,1,0:T(8,128)(2,1)}, u32[]{:S(2)}) copy-start(bf16[2,32,256]{2,1,0:T(8,128)(2,1)} %kernels_ref.1) | copy-start | bytes 98308

commit v2 on v1

--- a/solution.py
+++ b/solution.py
@@ -45,9 +45,33 @@
     return jnp.concatenate(parts, axis=0).astype(jnp.bfloat16)
 
 
-def partial_series(tm_count, chan_count, samples_ref, delay_ref, tail_ref, out_ref, moved, chosen):
+def partial_series(
+    tm_count,
+    chan_count,
+    samples_hbm,
+    delay_hbm,
+    tail_hbm,
+    out_ref,
+    samples_ref,
+    delay_ref,
+    tail_ref,
+    moved,
+    chosen,
+    arrived,
+):
     channels, block_len = samples_ref.shape
     trials = tail_ref.shape[1]
+    copies = [
+        pltpu.make_async_copy(source, target, arrived.at[index])
+        for index, (source, target) in enumerate(
+            [(delay_hbm, delay_ref), (tail_hbm, tail_ref), (samples_hbm, samples_ref)]
+        )
+    ]
+    for copy in copies:
+        copy.start()
+    out_ref[...] = jnp.zeros_like(out_ref)
+    for copy in copies:
+        copy.wait()
     samples = samples_ref[...]
     padded = jnp.concatenate([jnp.zeros((channels, LANES), jnp.bfloat16), samples], axis=1)
     for coarse in range(COARSE):
@@ -112,7 +136,6 @@
 
     group_rows = chan_count * ROWS
     group = lax.axis_index("tm")
-    out_ref[...] = jnp.zeros_like(out_ref)
     out_ref[pl.ds(pl.multiple_of(group * group_rows, group_rows), group_rows), :] = trial_blocks(
         late, chan_count
     )
@@ -177,13 +200,27 @@
     parts = pl.pallas_call(
         functools.partial(partial_series, tm_count, chan_count),
         out_shape=jax.ShapeDtypeStruct((devices * ROWS, LANES), jnp.bfloat16),
+        in_specs=[pl.BlockSpec(memory_space=pltpu.HBM)] * 3,
         scratch_shapes=[
+            pltpu.VMEM((channels, block_len), jnp.bfloat16),
+            pltpu.VMEM((chan_count, channels), jnp.int32),
+            pltpu.VMEM((1, trials), jnp.int32),
             pltpu.VMEM((COARSE * channels, block_len + LANES), jnp.bfloat16),
             pltpu.VMEM((2 * FINE * trials, COARSE * channels), jnp.bfloat16),
+            pltpu.SemaphoreType.DMA((3,)),
         ],
         compiler_params=pltpu.CompilerParams(vmem_limit_bytes=40 * 1024 * 1024),
         name="partial_series",
-    )(filterbank, chan_delay.reshape(chan_count, channels), tail_len.reshape(1, trials))
+    )(
+        *(
+            pltpu.with_memory_space_constraint(value, pltpu.HBM)
+            for value in (
+                filterbank,
+                chan_delay.reshape(chan_count, channels),
+                tail_len.reshape(1, trials),
+            )
+        )
+    )
     parts = lax.all_to_all(parts, ("tm", "chan"), 0, 0, tiled=True)
     return pl.pallas_call(
         functools.partial(accel_search, tm_count, chan_count),

time: 20 us -> 18.7 us (0.935)
  local copies, waits for them, and re-layouts: 2.19 us -> 0.01 us
  Pallas kernels: 3.19 us -> 4.09 us
    unnamed x10 -> x4, local copies, waits for them, and re-layouts: 2.19 us -> 0.01 us
    pallas_call x1, Pallas kernels: 1.75 us -> 2.66 us  [shards(): pl.pallas_call(functools.partial(partial_series, tm_count, chan_count), o...]
where the time goes in v2:
time: 18.7 us; the launch traced here: 18.5 us
  blocking collectives  14.4 us (77%)
  Pallas kernels  4.09 us (22%)
    all_to_all x1, blocking collectives, shards(): parts = lax.all_to_all(parts, ('tm', 'chan'), 0, 0, tiled=True)  14.4 us
    pallas_call x1, Pallas kernels, shards(): pl.pallas_call(functools.partial(partial_series, tm_count, chan_count), o...  2.66 us
    pallas_call x1, Pallas kernels, shards(): pl.pallas_call(functools.partial(accel_search, tm_count, chan_count), out...  1.43 us

profile of v2, /device:TPU:0, one launch (start us, length us, event | category | flops | bytes accessed | tf_op | source)
XLA Modules:
  0.0 18.5 jit_solution(1759105161160000601)
XLA Ops:
  0.0 2.7 %partial_series.1 = bf16[256,128]{1,0:T(8,128)(2,1)S(1)} custom-call(bf16[128,256]{1,0:T(8,128)(2,1)} %samples_hbm.1, s32[8,128]{1,0:T(8,128)} %bitcast.6, s32[1,32]{1,0:T(1,128)} %bitcast.7), custom_call_target="tpu_custom_call" | custom-call | tf_op jit(solution)/shard_map/partial_series/pallas_call | solution.py:200
  2.7 0.0 copy-start
  2.7 0.0 copy-start.1
  2.7 14.4 %all_to_all.11 = bf16[32,8,128]{2,1,0:T(8,128)(2,1)S(1)} all-to-all(bf16[32,8,128]{2,1,0:T(8,128)(2,1)S(1)} %bitcast.5), channel_id=1, replica_groups=mesh['tm'=4,'chan'=8] {'tm','chan'}, dimensions={0} | all-to-all | bytes 131072 | tf_op jit(solution)/shard_map/all_to_all | solution.py:224
  17.1 0.0 copy-done
  17.1 0.0 copy-done.1
  17.1 1.4 %accel_search.1 = bf16[32,4,128]{2,1,0:T(4,128)(2,1)} custom-call(bf16[256,128]{1,0:T(8,128)(2,1)S(1)} %bitcast.4, bf16[128,256]{1,0:T(8,128)(2,1)S(1)} %copy-done, bf16[2,32,256]{2,1,0:T(8,128)(2,1)S(1)} %copy-done.1), custom_call_target="tpu_custom_call" | custom-call | tf_op jit(solution)/shard_map/accel_search/pallas_call | solution.py:225
Async XLA Ops:
  2.7 14.4 %copy-start = (bf16[128,256]{1,0:T(8,128)(2,1)S(1)}, bf16[128,256]{1,0:T(8,128)(2,1)}, u32[]{:S(2)}) copy-start(bf16[128,256]{1,0:T(8,128)(2,1)} %constant.2.clone.table_ref) | copy-start | bytes 196612
  2.7 14.4 %copy-start.1 = (bf16[2,32,256]{2,1,0:T(8,128)(2,1)S(1)}, bf16[2,32,256]{2,1,0:T(8,128)(2,1)}, u32[]{:S(2)}) copy-start(bf16[2,32,256]{2,1,0:T(8,128)(2,1)} %kernels_ref.1) | copy-start | bytes 98308

commit v3 on v2

--- a/solution.py
+++ b/solution.py
@@ -12,8 +12,7 @@
 TRIAL_DEV = 4
 MAXDELAY = 4096
 LANES = 128
-FINE = 16
-COARSE = LANES // FINE
+STEP = 8
 ROWS = 2 * TRIAL_DEV
 
 
@@ -34,7 +33,7 @@
     count = row.shape[1]
     rows = lax.broadcasted_iota(jnp.int32, (count, count), 0)
     columns = lax.broadcasted_iota(jnp.int32, (count, count), 1)
-    return jnp.sum(jnp.where(rows == columns, row, 0), axis=1, keepdims=True)
+    return jnp.sum(jnp.where(rows == columns, row, 0.0), axis=1, keepdims=True)
 
 
 def trial_blocks(value, chan_count):
@@ -55,12 +54,18 @@
     samples_ref,
     delay_ref,
     tail_ref,
+    turned,
     moved,
     chosen,
+    total,
     arrived,
 ):
     channels, block_len = samples_ref.shape
     trials = tail_ref.shape[1]
+    repeats = max(1, LANES // trials)
+    width = repeats * trials
+    groups = block_len // (STEP * repeats)
+    pair = max(1, 2 * LANES // width)
     copies = [
         pltpu.make_async_copy(source, target, arrived.at[index])
         for index, (source, target) in enumerate(
@@ -70,80 +75,86 @@
     for copy in copies:
         copy.start()
     out_ref[...] = jnp.zeros_like(out_ref)
-    for copy in copies:
-        copy.wait()
-    samples = samples_ref[...]
-    padded = jnp.concatenate([jnp.zeros((channels, LANES), jnp.bfloat16), samples], axis=1)
-    for coarse in range(COARSE):
-        moved[coarse * channels : (coarse + 1) * channels, :] = (
-            shift_left(padded, FINE * coarse) if coarse else padded
-        )
-
-    delays = delay_ref[pl.ds(lax.axis_index("chan"), 1), :]
-    tails = as_column(tail_ref[...])
-    shifts = lax.shift_right_logical(delays * tails, MAXDELAY.bit_length() - 1)
-    shift_vals = shifts.astype(jnp.float32)
-    rests = jnp.concatenate([shift_vals - FINE * coarse for coarse in range(COARSE)], axis=1)
-    rests = rests.astype(jnp.bfloat16)
+    copies[0].wait()
+    copies[1].wait()
+
+    delays = as_column(delay_ref[pl.ds(lax.axis_index("chan"), 1), :].astype(jnp.float32))
+    tails = jnp.concatenate([tail_ref[...].astype(jnp.float32)] * repeats, axis=1)
+    shifts = jnp.floor(delays * tails * (1.0 / MAXDELAY))
+    columns = lax.broadcasted_iota(jnp.int32, (channels, width), 1)
+    rests = (shifts - STEP * (columns // trials).astype(jnp.float32)).astype(jnp.bfloat16)
     one = jnp.ones((), jnp.bfloat16)
     zero = jnp.zeros((), jnp.bfloat16)
-    for part in range(2):
-        for fine in range(FINE):
-            first = (part * FINE + fine) * trials
-            wanted = jnp.array(part * LANES + fine, jnp.bfloat16)
-            chosen[first : first + trials, :] = jnp.where(rests == wanted, one, zero)
-    sums = jnp.dot(chosen[...], moved[...], preferred_element_type=jnp.float32)
-
-    level = []
-    for fine in range(FINE):
-        near = sums[fine * trials : (fine + 1) * trials]
-        far = sums[(FINE + fine) * trials : (FINE + fine + 1) * trials]
-        level.append(
-            jnp.concatenate(
-                [
-                    far[:, :LANES],
-                    far[:, LANES : 2 * LANES] + near[:, :LANES],
-                    far[:, 2 * LANES :] + near[:, LANES : 2 * LANES],
-                    near[:, 2 * LANES :],
-                ],
-                axis=1,
-            )
-        )
-    steps = 1
-    while len(level) > 1:
-        level = [
-            level[2 * i] + shift_left(level[2 * i + 1], steps) for i in range(len(level) // 2)
-        ]
-        steps *= 2
-    series = level[0]
-
-    rows = lax.broadcasted_iota(jnp.int32, (block_len, LANES), 0)
-    columns = lax.broadcasted_iota(jnp.int32, (block_len, LANES), 1)
+
+    def where_rest_is(value):
+        return jnp.where(rests == jnp.array(value, jnp.bfloat16), one, zero)
+
+    def choose(first):
+        for fine in range(STEP):
+            for group in range(first, min(first + pair, groups)):
+                chosen[
+                    fine * channels : (fine + 1) * channels, group * width : (group + 1) * width
+                ] = where_rest_is(STEP * repeats * group + fine)
+
+    choose(0)
+    whole = where_rest_is(block_len)
+    parity = jnp.where(shifts - 2.0 * jnp.floor(shifts * 0.5) == 0.0, one, -one)
+
+    copies[2].wait()
+    rows = moved.shape[0]
+    turned[:STEP] = jnp.zeros((STEP, channels), jnp.float32)
+    turned[STEP : STEP + block_len] = samples_ref[...].astype(jnp.float32).T
+    turned[STEP + block_len :] = jnp.zeros((2 * STEP, channels), jnp.float32)
+    for fine in range(STEP):
+        moved[:, fine * channels : (fine + 1) * channels] = turned[fine : fine + rows].astype(
+            jnp.bfloat16
+        )
+    unmoved = moved[:, :channels]
+    whole_sums = jnp.dot(unmoved, whole, preferred_element_type=jnp.float32)
+    signs = lax.broadcasted_iota(jnp.int32, (STEP, rows), 0)
+    signs += lax.broadcasted_iota(jnp.int32, (STEP, rows), 1)
     nyquist_step = 0.5 / block_len
-    alternating = jnp.where((rows + columns) % 2 == 0, -nyquist_step, nyquist_step)
-    nyquist = jnp.dot(samples, alternating.astype(jnp.bfloat16), preferred_element_type=jnp.float32)
-    parity = jnp.where(shifts % 2 == 0, 1.0, -1.0).astype(jnp.bfloat16)
-    top_bin = jnp.dot(parity, nyquist.astype(jnp.bfloat16), preferred_element_type=jnp.float32)
-    top_bin = jnp.concatenate([top_bin, top_bin], axis=1)
-    whole = jnp.where(shifts == block_len, 1.0, 0.0).astype(jnp.bfloat16)
-    whole_block = jnp.dot(whole, samples, preferred_element_type=jnp.float32)
-
-    scale = 1.0 / math.sqrt(channels * chan_count)
-    late = (series[:, block_len:] + top_bin) * scale
-    early = (series[:, :block_len] + top_bin + whole_block) * scale
-    positions = lax.broadcasted_iota(jnp.int32, (trials, block_len), 1)
-    early = jnp.where(positions >= block_len - tails, early, 0.0)
+    alternating = jnp.where(signs % 2 == 0, -nyquist_step, nyquist_step).astype(jnp.bfloat16)
+    nyquist = jnp.dot(alternating, unmoved, preferred_element_type=jnp.float32)
+    top_bin = jnp.dot(nyquist.astype(jnp.bfloat16), parity, preferred_element_type=jnp.float32)
+    top_bin = jnp.where(columns[:STEP] < trials, top_bin, 0.0)
+
+    sublanes = lax.broadcasted_iota(jnp.int32, (STEP, width), 0)
+    chunks = block_len // STEP
+    for chunk in range(2 * chunks):
+        start = top_bin
+        if chunk < chunks:
+            positions = (sublanes + chunk * STEP).astype(jnp.float32)
+            start = jnp.where(positions >= block_len - tails, top_bin, 0.0)
+            start += whole_sums[(chunk + 1) * STEP : (chunk + 2) * STEP]
+        total[chunk * STEP : (chunk + 1) * STEP] = start
+    for first in range(0, groups, pair):
+        if first + pair < groups:
+            choose(first + pair)
+        last = min(first + pair, groups)
+        sums = jnp.dot(
+            moved[...], chosen[:, first * width : last * width], preferred_element_type=jnp.float32
+        )
+        for group in range(first, last):
+            start = block_len - STEP - STEP * repeats * group
+            columns_of = slice((group - first) * width, (group - first + 1) * width)
+            total[start : start + block_len + STEP] += sums[: block_len + STEP, columns_of]
+    turned_back = total[...].T
+    series = turned_back[:trials]
+    for repeat in range(1, repeats):
+        series += shift_left(turned_back[repeat * trials : (repeat + 1) * trials], repeat * STEP)
+    series *= 1.0 / math.sqrt(channels * chan_count)
 
     group_rows = chan_count * ROWS
     group = lax.axis_index("tm")
     out_ref[pl.ds(pl.multiple_of(group * group_rows, group_rows), group_rows), :] = trial_blocks(
-        late, chan_count
+        series[:, block_len:], chan_count
     )
 
     @pl.when(group > 0)
     def _():
         before = pl.multiple_of((group - 1) * group_rows, group_rows)
-        out_ref[pl.ds(before, group_rows), :] = trial_blocks(early, chan_count)
+        out_ref[pl.ds(before, group_rows), :] = trial_blocks(series[:, :block_len], chan_count)
 
 
 def accel_search(tm_count, chan_count, parts_ref, table_ref, kernels_ref, out_ref):
@@ -205,8 +216,10 @@
             pltpu.VMEM((channels, block_len), jnp.bfloat16),
             pltpu.VMEM((chan_count, channels), jnp.int32),
             pltpu.VMEM((1, trials), jnp.int32),
-            pltpu.VMEM((COARSE * channels, block_len + LANES), jnp.bfloat16),
-            pltpu.VMEM((2 * FINE * trials, COARSE * channels), jnp.bfloat16),
+            pltpu.VMEM((block_len + 3 * STEP, channels), jnp.float32),
+            pltpu.VMEM((block_len + 2 * STEP, STEP * channels), jnp.bfloat16),
+            pltpu.VMEM((STEP * channels, block_len // STEP * trials), jnp.bfloat16),
+            pltpu.VMEM((2 * block_len, max(LANES, trials)), jnp.float32),
             pltpu.SemaphoreType.DMA((3,)),
         ],
         compiler_params=pltpu.CompilerParams(vmem_limit_bytes=40 * 1024 * 1024),

time: 18.7 us -> 18.3 us (0.979)
  Pallas kernels: 4.09 us -> 3.67 us
    pallas_call x1, Pallas kernels: 2.66 us -> 2.23 us  [shards(): pl.pallas_call(functools.partial(partial_series, tm_count, chan_count), o...]
where the time goes in v3:
time: 18.3 us; the launch traced here: 18.1 us
  blocking collectives  14.4 us (79%)
  Pallas kernels  3.67 us (20%)
    all_to_all x1, blocking collectives, shards(): parts = lax.all_to_all(parts, ('tm', 'chan'), 0, 0, tiled=True)  14.4 us
    pallas_call x1, Pallas kernels, shards(): pl.pallas_call(functools.partial(partial_series, tm_count, chan_count), o...  2.23 us
    pallas_call x1, Pallas kernels, shards(): pl.pallas_call(functools.partial(accel_search, tm_count, chan_count), out...  1.44 us

profile of v3, /device:TPU:0, one launch (start us, length us, event | category | flops | bytes accessed | tf_op | source)
XLA Modules:
  0.0 18.1 jit_solution(18237695652411445293)
XLA Ops:
  0.0 2.2 %partial_series.1 = bf16[256,128]{1,0:T(8,128)(2,1)S(1)} custom-call(bf16[128,256]{1,0:T(8,128)(2,1)} %samples_hbm.1, s32[8,128]{1,0:T(8,128)} %bitcast.6, s32[1,32]{1,0:T(1,128)} %bitcast.7), custom_call_target="tpu_custom_call" | custom-call | tf_op jit(solution)/shard_map/partial_series/pallas_call | solution.py:211
  2.2 0.0 copy-start
  2.3 0.0 copy-start.1
  2.3 14.4 %all_to_all.11 = bf16[32,8,128]{2,1,0:T(8,128)(2,1)S(1)} all-to-all(bf16[32,8,128]{2,1,0:T(8,128)(2,1)S(1)} %bitcast.5), channel_id=1, replica_groups=mesh['tm'=4,'chan'=8] {'tm','chan'}, dimensions={0} | all-to-all | bytes 131072 | tf_op jit(solution)/shard_map/all_to_all | solution.py:237
  16.7 0.0 copy-done
  16.7 0.0 copy-done.1
  16.7 1.4 %accel_search.1 = bf16[32,4,128]{2,1,0:T(4,128)(2,1)} custom-call(bf16[256,128]{1,0:T(8,128)(2,1)S(1)} %bitcast.4, bf16[128,256]{1,0:T(8,128)(2,1)S(1)} %copy-done, bf16[2,32,256]{2,1,0:T(8,128)(2,1)S(1)} %copy-done.1), custom_call_target="tpu_custom_call" | custom-call | tf_op jit(solution)/shard_map/accel_search/pallas_call | solution.py:238
Async XLA Ops:
  2.2 14.4 %copy-start = (bf16[128,256]{1,0:T(8,128)(2,1)S(1)}, bf16[128,256]{1,0:T(8,128)(2,1)}, u32[]{:S(2)}) copy-start(bf16[128,256]{1,0:T(8,128)(2,1)} %constant.2.clone.table_ref) | copy-start | bytes 196612
  2.3 14.4 %copy-start.1 = (bf16[2,32,256]{2,1,0:T(8,128)(2,1)S(1)}, bf16[2,32,256]{2,1,0:T(8,128)(2,1)}, u32[]{:S(2)}) copy-start(bf16[2,32,256]{2,1,0:T(8,128)(2,1)} %kernels_ref.1) | copy-start | bytes 98308

commit v4 on v3

--- a/solution.py
+++ b/solution.py
@@ -157,7 +157,9 @@
         out_ref[pl.ds(before, group_rows), :] = trial_blocks(series[:, :block_len], chan_count)
 
 
-def accel_search(tm_count, chan_count, parts_ref, table_ref, kernels_ref, out_ref):
+def accel_search(
+    tm_count, chan_count, parts_ref, table_ref, reverse_ref, kernels_ref, out_ref, windows, by_kernel
+):
     group_rows = chan_count * ROWS
     group = lax.axis_index("tm")
     after = lax.rem(group + 1, tm_count)
@@ -174,33 +176,40 @@
     spectra = (halves[:TRIAL_DEV] + signs * halves[TRIAL_DEV:]) * (1.0 / math.sqrt(block_len))
     spectra = spectra.astype(jnp.bfloat16).astype(jnp.float32)
 
-    sublanes = lax.broadcasted_iota(jnp.int32, (8, block_len), 0)
-    zeros = jnp.zeros((8, half_len), jnp.float32)
-    taps = []
+    taps = lax.broadcasted_iota(jnp.int32, (half_len, half_len), 0)
+    bins = lax.broadcasted_iota(jnp.int32, (half_len, half_len), 1)
+    early = bins <= taps
+    zero = jnp.zeros((), jnp.bfloat16)
     for trial in range(TRIAL_DEV):
-        windows = []
-        for first in (0, half_len):
-            row = spectra[trial : trial + 1, first : first + half_len]
-            wide = jnp.concatenate([zeros, jnp.broadcast_to(row, (8, half_len))], axis=1)
-            for steps in (1, 2, 4):
-                wide = jnp.where(sublanes & steps != 0, shift_left(wide, steps), wide)
-            for start in range(0, block_len, 8):
-                windows.append((shift_left(wide, start) if start else wide)[:, :half_len])
-        taps.append(jnp.concatenate(windows, axis=0).astype(jnp.bfloat16))
-    windows = jnp.concatenate(taps, axis=1)
-
-    real = kernels_ref[0]
-    imag = kernels_ref[1]
+        for part in range(2):
+            row = spectra[trial : trial + 1, part * half_len : (part + 1) * half_len]
+            turned = pltpu.roll(
+                jnp.broadcast_to(row, (half_len, half_len)), 1, 1, stride=1, stride_axis=0
+            ).astype(jnp.bfloat16)
+            first = part * block_len
+            columns_of = slice(trial * half_len, (trial + 1) * half_len)
+            windows[first : first + half_len, columns_of] = jnp.where(early, turned, zero)
+            windows[first + half_len : first + block_len, columns_of] = jnp.where(
+                early, zero, turned
+            )
+
+    real, imag = (
+        jnp.dot(kernels_ref[part], reverse_ref[...], preferred_element_type=jnp.float32).astype(
+            jnp.bfloat16
+        )
+        for part in range(2)
+    )
     weights = jnp.concatenate(
         [jnp.concatenate([real, -imag], axis=1), jnp.concatenate([imag, real], axis=1)], axis=0
     )
-    correlation = jnp.dot(weights, windows, preferred_element_type=jnp.float32)
+    correlation = jnp.dot(weights, windows[...], preferred_element_type=jnp.float32)
     accels = real.shape[0]
     power = correlation[:accels] * correlation[:accels] + correlation[accels:] * correlation[accels:]
     for trial in range(TRIAL_DEV):
-        out_ref[:, trial, :] = power[:, trial * half_len : (trial + 1) * half_len].astype(
-            jnp.bfloat16
-        )
+        by_kernel[pl.ds(trial, accels, stride=TRIAL_DEV), :] = power[
+            :, trial * half_len : (trial + 1) * half_len
+        ]
+    out_ref[...] = by_kernel[...].astype(jnp.bfloat16)
 
 
 def shards(tm_count, chan_count, filterbank, chan_delay, tail_len, kernels):
@@ -235,12 +244,18 @@
         )
     )
     parts = lax.all_to_all(parts, ("tm", "chan"), 0, 0, tiled=True)
-    return pl.pallas_call(
+    reverse = jnp.asarray(np.eye(block_len, dtype=np.float32)[::-1], jnp.bfloat16)
+    power = pl.pallas_call(
         functools.partial(accel_search, tm_count, chan_count),
-        out_shape=jax.ShapeDtypeStruct((accels, TRIAL_DEV, block_len // 2), jnp.bfloat16),
+        out_shape=jax.ShapeDtypeStruct((accels * TRIAL_DEV, block_len // 2), jnp.bfloat16),
+        scratch_shapes=[
+            pltpu.VMEM((2 * block_len, TRIAL_DEV * block_len // 2), jnp.bfloat16),
+            pltpu.VMEM((accels * TRIAL_DEV, block_len // 2), jnp.float32),
+        ],
         compiler_params=pltpu.CompilerParams(vmem_limit_bytes=40 * 1024 * 1024),
         name="accel_search",
-    )(parts, bin_table(block_len), kernels)
+    )(parts, bin_table(block_len), reverse, kernels)
+    return power.reshape(accels, TRIAL_DEV, block_len // 2)
 
 
 def solution(mesh):

time: 18.3 us -> 18 us (0.984)
  Pallas kernels: 3.67 us -> 3.37 us
    pallas_call x1, Pallas kernels: 1.44 us -> 1.1 us  [shards(): pl.pallas_call(functools.partial(accel_search, tm_count, chan_count), out...]
where the time goes in v4:
time: 18 us; the launch traced here: 17.8 us
  blocking collectives  14.4 us (80%)
  Pallas kernels  3.37 us (19%)
    all_to_all x1, blocking collectives, shards(): parts = lax.all_to_all(parts, ('tm', 'chan'), 0, 0, tiled=True)  14.4 us
    pallas_call x1, Pallas kernels, shards(): pl.pallas_call(functools.partial(partial_series, tm_count, chan_count), o...  2.27 us
    pallas_call x1, Pallas kernels, shards(): pl.pallas_call(functools.partial(accel_search, tm_count, chan_count), out...  1.1 us

profile of v4, /device:TPU:0, one launch (start us, length us, event | category | flops | bytes accessed | tf_op | source)
XLA Modules:
  0.0 17.8 jit_solution(9598121142321111791)
XLA Ops:
  0.0 0.0 copy-start
  0.0 2.3 %partial_series.1 = bf16[256,128]{1,0:T(8,128)(2,1)S(1)} custom-call(bf16[128,256]{1,0:T(8,128)(2,1)} %samples_hbm.1, s32[8,128]{1,0:T(8,128)} %bitcast.7, s32[1,32]{1,0:T(1,128)} %bitcast.8), custom_call_target="tpu_custom_call" | custom-call | tf_op jit(solution)/shard_map/partial_series/pallas_call | solution.py:220
  2.3 0.0 copy-start.1
  2.3 0.0 copy-start.2
  2.3 14.4 %all_to_all.11 = bf16[32,8,128]{2,1,0:T(8,128)(2,1)S(1)} all-to-all(bf16[32,8,128]{2,1,0:T(8,128)(2,1)S(1)} %bitcast.6), channel_id=1, replica_groups=mesh['tm'=4,'chan'=8] {'tm','chan'}, dimensions={0} | all-to-all | bytes 131072 | tf_op jit(solution)/shard_map/all_to_all | solution.py:246
  16.7 0.0 copy-done
  16.7 0.0 copy-done.1
  16.7 0.0 copy-done.2
  16.7 1.1 %accel_search.1 = bf16[128,128]{1,0:T(8,128)(2,1)} custom-call(bf16[256,128]{1,0:T(8,128)(2,1)S(1)} %bitcast.5, bf16[128,256]{1,0:T(8,128)(2,1)S(1)} %copy-done.1, bf16[256,256]{1,0:T(8,128)(2,1)S(1)} %copy-done, bf16[2,32,256]{2,1,0:T(8,128)(2,1)S(1)} %copy-done.2), custom_call_target="tpu_custom_call" | custom-call | tf_op jit(solution)/shard_map/accel_search/pallas_call | solution.py:248
Async XLA Ops:
  0.0 16.7 %copy-start = (bf16[256,256]{1,0:T(8,128)(2,1)S(1)}, bf16[256,256]{1,0:T(8,128)(2,1)}, u32[]{:S(2)}) copy-start(bf16[256,256]{1,0:T(8,128)(2,1)} %constant.4.clone.reverse_ref) | copy-start | bytes 393220
  2.3 14.4 %copy-start.1 = (bf16[128,256]{1,0:T(8,128)(2,1)S(1)}, bf16[128,256]{1,0:T(8,128)(2,1)}, u32[]{:S(2)}) copy-start(bf16[128,256]{1,0:T(8,128)(2,1)} %constant.5.clone.table_ref) | copy-start | bytes 196612
  2.3 14.4 %copy-start.2 = (bf16[2,32,256]{2,1,0:T(8,128)(2,1)S(1)}, bf16[2,32,256]{2,1,0:T(8,128)(2,1)}, u32[]{:S(2)}) copy-start(bf16[2,32,256]{2,1,0:T(8,128)(2,1)} %kernels_ref.1) | copy-start | bytes 98308

commit v5 on v4

--- a/solution.py
+++ b/solution.py
@@ -82,7 +82,8 @@
     tails = jnp.concatenate([tail_ref[...].astype(jnp.float32)] * repeats, axis=1)
     shifts = jnp.floor(delays * tails * (1.0 / MAXDELAY))
     columns = lax.broadcasted_iota(jnp.int32, (channels, width), 1)
-    rests = (shifts - STEP * (columns // trials).astype(jnp.float32)).astype(jnp.bfloat16)
+    repeat_of = columns // trials
+    rests = (shifts - STEP * groups * repeat_of.astype(jnp.float32)).astype(jnp.bfloat16)
     one = jnp.ones((), jnp.bfloat16)
     zero = jnp.zeros((), jnp.bfloat16)
 
@@ -94,40 +95,23 @@
             for group in range(first, min(first + pair, groups)):
                 chosen[
                     fine * channels : (fine + 1) * channels, group * width : (group + 1) * width
-                ] = where_rest_is(STEP * repeats * group + fine)
+                ] = where_rest_is(STEP * group + fine)
 
     choose(0)
-    whole = where_rest_is(block_len)
-    parity = jnp.where(shifts - 2.0 * jnp.floor(shifts * 0.5) == 0.0, one, -one)
+    own_shifts = shifts[:, :trials]
+    whole = jnp.where(own_shifts == block_len, one, zero)
+    parity = jnp.where(own_shifts - 2.0 * jnp.floor(own_shifts * 0.5) == 0.0, one, -one)
 
     copies[2].wait()
     rows = moved.shape[0]
     turned[:STEP] = jnp.zeros((STEP, channels), jnp.float32)
-    turned[STEP : STEP + block_len] = samples_ref[...].astype(jnp.float32).T
+    turned[STEP : STEP + block_len] = samples_ref[...].T.astype(jnp.float32)
     turned[STEP + block_len :] = jnp.zeros((2 * STEP, channels), jnp.float32)
     for fine in range(STEP):
         moved[:, fine * channels : (fine + 1) * channels] = turned[fine : fine + rows].astype(
             jnp.bfloat16
         )
-    unmoved = moved[:, :channels]
-    whole_sums = jnp.dot(unmoved, whole, preferred_element_type=jnp.float32)
-    signs = lax.broadcasted_iota(jnp.int32, (STEP, rows), 0)
-    signs += lax.broadcasted_iota(jnp.int32, (STEP, rows), 1)
-    nyquist_step = 0.5 / block_len
-    alternating = jnp.where(signs % 2 == 0, -nyquist_step, nyquist_step).astype(jnp.bfloat16)
-    nyquist = jnp.dot(alternating, unmoved, preferred_element_type=jnp.float32)
-    top_bin = jnp.dot(nyquist.astype(jnp.bfloat16), parity, preferred_element_type=jnp.float32)
-    top_bin = jnp.where(columns[:STEP] < trials, top_bin, 0.0)
-
-    sublanes = lax.broadcasted_iota(jnp.int32, (STEP, width), 0)
-    chunks = block_len // STEP
-    for chunk in range(2 * chunks):
-        start = top_bin
-        if chunk < chunks:
-            positions = (sublanes + chunk * STEP).astype(jnp.float32)
-            start = jnp.where(positions >= block_len - tails, top_bin, 0.0)
-            start += whole_sums[(chunk + 1) * STEP : (chunk + 2) * STEP]
-        total[chunk * STEP : (chunk + 1) * STEP] = start
+    total[...] = jnp.zeros_like(total)
     for first in range(0, groups, pair):
         if first + pair < groups:
             choose(first + pair)
@@ -136,25 +120,50 @@
             moved[...], chosen[:, first * width : last * width], preferred_element_type=jnp.float32
         )
         for group in range(first, last):
-            start = block_len - STEP - STEP * repeats * group
+            start = STEP * (groups - 1 - group)
             columns_of = slice((group - first) * width, (group - first + 1) * width)
             total[start : start + block_len + STEP] += sums[: block_len + STEP, columns_of]
+    signs = lax.broadcasted_iota(jnp.int32, (block_len, block_len), 0)
+    signs += lax.broadcasted_iota(jnp.int32, (block_len, block_len), 1)
+    nyquist_step = 0.5 / block_len
+    alternating = jnp.where(signs % 2 == 0, -nyquist_step, nyquist_step).astype(jnp.bfloat16)
+    samples = samples_ref[...]
+    nyquist = jnp.dot(samples, alternating, preferred_element_type=jnp.float32)
+    over_channels = (((0,), (0,)), ((), ()))
+    top_bin = lax.dot_general(
+        parity, nyquist.astype(jnp.bfloat16), over_channels, preferred_element_type=jnp.float32
+    )
+    whole_block = lax.dot_general(
+        whole, samples, over_channels, preferred_element_type=jnp.float32
+    )
     turned_back = total[...].T
-    series = turned_back[:trials]
-    for repeat in range(1, repeats):
-        series += shift_left(turned_back[repeat * trials : (repeat + 1) * trials], repeat * STEP)
-    series *= 1.0 / math.sqrt(channels * chan_count)
+    sums_by_rest = {}
+    for repeat in range(repeats):
+        part = turned_back[repeat * trials : (repeat + 1) * trials]
+        offset = block_len - STEP * groups * (repeat + 1)
+        before = offset // LANES * LANES
+        after = 2 * block_len - before - part.shape[1]
+        if before:
+            part = jnp.concatenate([jnp.zeros((trials, before), jnp.float32), part], axis=1)
+        if after > 0:
+            part = jnp.concatenate([part, jnp.zeros((trials, after), jnp.float32)], axis=1)
+        part = part[:, : 2 * block_len]
+        rest = offset - before
+        sums_by_rest[rest] = sums_by_rest[rest] + part if rest in sums_by_rest else part
+    series = sum(pltpu.roll(part, rest, 1) if rest else part for rest, part in sums_by_rest.items())
+    scale = 1.0 / math.sqrt(channels * chan_count)
+    positions = lax.broadcasted_iota(jnp.int32, (trials, block_len), 1)
+    late = (series[:, block_len:] + top_bin) * scale
+    kept = positions.astype(jnp.float32) >= block_len - as_column(tails[:, :trials])
+    group = lax.axis_index("tm")
+    kept = jnp.logical_and(kept, group > 0)
+    early = jnp.where(kept, series[:, :block_len] + top_bin + whole_block, 0.0) * scale
 
     group_rows = chan_count * ROWS
-    group = lax.axis_index("tm")
-    out_ref[pl.ds(pl.multiple_of(group * group_rows, group_rows), group_rows), :] = trial_blocks(
-        series[:, block_len:], chan_count
-    )
-
-    @pl.when(group > 0)
-    def _():
-        before = pl.multiple_of((group - 1) * group_rows, group_rows)
-        out_ref[pl.ds(before, group_rows), :] = trial_blocks(series[:, :block_len], chan_count)
+    before = lax.rem(group + tm_count - 1, tm_count)
+    for target, value in ((group, late), (before, early)):
+        first = pl.multiple_of(target * group_rows, group_rows)
+        out_ref[pl.ds(first, group_rows), :] = trial_blocks(value, chan_count)
 
 
 def accel_search(
@@ -217,6 +226,8 @@
     trials = tail_len.shape[0]
     accels = kernels.shape[1]
     devices = tm_count * chan_count
+    total_rows = block_len + block_len // max(1, LANES // trials)
+    total_rows = -(-total_rows // LANES) * LANES
     parts = pl.pallas_call(
         functools.partial(partial_series, tm_count, chan_count),
         out_shape=jax.ShapeDtypeStruct((devices * ROWS, LANES), jnp.bfloat16),
@@ -228,7 +239,7 @@
             pltpu.VMEM((block_len + 3 * STEP, channels), jnp.float32),
             pltpu.VMEM((block_len + 2 * STEP, STEP * channels), jnp.bfloat16),
             pltpu.VMEM((STEP * channels, block_len // STEP * trials), jnp.bfloat16),
-            pltpu.VMEM((2 * block_len, max(LANES, trials)), jnp.float32),
+            pltpu.VMEM((total_rows, max(LANES, trials)), jnp.float32),
             pltpu.SemaphoreType.DMA((3,)),
         ],
         compiler_params=pltpu.CompilerParams(vmem_limit_bytes=40 * 1024 * 1024),

time: 18 us -> 17.8 us (0.989)
  Pallas kernels: 3.37 us -> 3.18 us
    pallas_call x1, Pallas kernels: 2.27 us -> 2.08 us  [shards(): pl.pallas_call(functools.partial(partial_series, tm_count, chan_count), o...]
where the time goes in v5:
time: 17.8 us; the launch traced here: 17.6 us
  blocking collectives  14.4 us (81%)
  Pallas kernels  3.18 us (18%)
    all_to_all x1, blocking collectives, shards(): parts = lax.all_to_all(parts, ('tm', 'chan'), 0, 0, tiled=True)  14.4 us
    pallas_call x1, Pallas kernels, shards(): pl.pallas_call(functools.partial(partial_series, tm_count, chan_count), o...  2.08 us
    pallas_call x1, Pallas kernels, shards(): pl.pallas_call(functools.partial(accel_search, tm_count, chan_count), out...  1.1 us

profile of v5, /device:TPU:0, one launch (start us, length us, event | category | flops | bytes accessed | tf_op | source)
XLA Modules:
  0.0 17.6 jit_solution(10353540338711990359)
XLA Ops:
  0.0 0.0 copy-start
  0.0 2.1 %partial_series.1 = bf16[256,128]{1,0:T(8,128)(2,1)S(1)} custom-call(bf16[128,256]{1,0:T(8,128)(2,1)} %samples_hbm.1, s32[8,128]{1,0:T(8,128)} %bitcast.7, s32[1,32]{1,0:T(1,128)} %bitcast.8), custom_call_target="tpu_custom_call" | custom-call | tf_op jit(solution)/shard_map/partial_series/pallas_call | solution.py:231
  2.1 0.0 copy-start.1
  2.1 0.0 copy-start.2
  2.1 14.4 %all_to_all.11 = bf16[32,8,128]{2,1,0:T(8,128)(2,1)S(1)} all-to-all(bf16[32,8,128]{2,1,0:T(8,128)(2,1)S(1)} %bitcast.6), channel_id=1, replica_groups=mesh['tm'=4,'chan'=8] {'tm','chan'}, dimensions={0} | all-to-all | bytes 131072 | tf_op jit(solution)/shard_map/all_to_all | solution.py:257
  16.5 0.0 copy-done
  16.5 0.0 copy-done.1
  16.5 0.0 copy-done.2
  16.5 1.1 %accel_search.1 = bf16[128,128]{1,0:T(8,128)(2,1)} custom-call(bf16[256,128]{1,0:T(8,128)(2,1)S(1)} %bitcast.5, bf16[128,256]{1,0:T(8,128)(2,1)S(1)} %copy-done.1, bf16[256,256]{1,0:T(8,128)(2,1)S(1)} %copy-done, bf16[2,32,256]{2,1,0:T(8,128)(2,1)S(1)} %copy-done.2), custom_call_target="tpu_custom_call" | custom-call | tf_op jit(solution)/shard_map/accel_search/pallas_call | solution.py:259
Async XLA Ops:
  0.0 16.5 %copy-start = (bf16[256,256]{1,0:T(8,128)(2,1)S(1)}, bf16[256,256]{1,0:T(8,128)(2,1)}, u32[]{:S(2)}) copy-start(bf16[256,256]{1,0:T(8,128)(2,1)} %constant.4.clone.reverse_ref) | copy-start | bytes 393220
  2.1 14.4 %copy-start.1 = (bf16[128,256]{1,0:T(8,128)(2,1)S(1)}, bf16[128,256]{1,0:T(8,128)(2,1)}, u32[]{:S(2)}) copy-start(bf16[128,256]{1,0:T(8,128)(2,1)} %constant.5.clone.table_ref) | copy-start | bytes 196612
  2.1 14.4 %copy-start.2 = (bf16[2,32,256]{2,1,0:T(8,128)(2,1)S(1)}, bf16[2,32,256]{2,1,0:T(8,128)(2,1)}, u32[]{:S(2)}) copy-start(bf16[2,32,256]{2,1,0:T(8,128)(2,1)} %kernels_ref.1) | copy-start | bytes 98308

commit v6 on v5

--- a/solution.py
+++ b/solution.py
@@ -97,7 +97,6 @@
                     fine * channels : (fine + 1) * channels, group * width : (group + 1) * width
                 ] = where_rest_is(STEP * group + fine)
 
-    choose(0)
     own_shifts = shifts[:, :trials]
     whole = jnp.where(own_shifts == block_len, one, zero)
     parity = jnp.where(own_shifts - 2.0 * jnp.floor(own_shifts * 0.5) == 0.0, one, -one)
@@ -111,10 +110,13 @@
         moved[:, fine * channels : (fine + 1) * channels] = turned[fine : fine + rows].astype(
             jnp.bfloat16
         )
-    total[...] = jnp.zeros_like(total)
+    filled = STEP * (groups - 1)
+    total[:filled] = jnp.zeros((filled, width), jnp.float32)
+    rest = total.shape[0] - filled - block_len - STEP
+    if rest:
+        total[filled + block_len + STEP :] = jnp.zeros((rest, width), jnp.float32)
     for first in range(0, groups, pair):
-        if first + pair < groups:
-            choose(first + pair)
+        choose(first)
         last = min(first + pair, groups)
         sums = jnp.dot(
             moved[...], chosen[:, first * width : last * width], preferred_element_type=jnp.float32
@@ -122,7 +124,11 @@
         for group in range(first, last):
             start = STEP * (groups - 1 - group)
             columns_of = slice((group - first) * width, (group - first + 1) * width)
-            total[start : start + block_len + STEP] += sums[: block_len + STEP, columns_of]
+            rows_of = slice(start, start + block_len + STEP)
+            if group == 0:
+                total[rows_of] = sums[: block_len + STEP, columns_of]
+            else:
+                total[rows_of] += sums[: block_len + STEP, columns_of]
     signs = lax.broadcasted_iota(jnp.int32, (block_len, block_len), 0)
     signs += lax.broadcasted_iota(jnp.int32, (block_len, block_len), 1)
     nyquist_step = 0.5 / block_len
@@ -161,7 +167,7 @@
 
     group_rows = chan_count * ROWS
     before = lax.rem(group + tm_count - 1, tm_count)
-    for target, value in ((group, late), (before, early)):
+    for target, value in ((group, late), (before, early))[: min(tm_count, 2)]:
         first = pl.multiple_of(target * group_rows, group_rows)
         out_ref[pl.ds(first, group_rows), :] = trial_blocks(value, chan_count)
 
@@ -173,8 +179,10 @@
     group = lax.axis_index("tm")
     after = lax.rem(group + 1, tm_count)
     own = parts_ref[pl.ds(pl.multiple_of(group * group_rows, group_rows), group_rows), :]
-    following = parts_ref[pl.ds(pl.multiple_of(after * group_rows, group_rows), group_rows), :]
-    both = own.astype(jnp.float32) + following.astype(jnp.float32)
+    both = own.astype(jnp.float32)
+    if tm_count > 1:
+        following = parts_ref[pl.ds(pl.multiple_of(after * group_rows, group_rows), group_rows), :]
+        both += following.astype(jnp.float32)
     series = jnp.sum(both.reshape(chan_count, ROWS, LANES), axis=0).astype(jnp.bfloat16)
 
     half_len = LANES

time: 17.8 us -> 17.7 us (level)
  no operation moved by 1% of the time
where the time goes in v6:
time: 17.7 us; the launch traced here: 17.6 us
  blocking collectives  14.4 us (81%)
  Pallas kernels  3.13 us (18%)
    all_to_all x1, blocking collectives, shards(): parts = lax.all_to_all(parts, ('tm', 'chan'), 0, 0, tiled=True)  14.4 us
    pallas_call x1, Pallas kernels, shards(): pl.pallas_call(functools.partial(partial_series, tm_count, chan_count), o...  2.03 us
    pallas_call x1, Pallas kernels, shards(): pl.pallas_call(functools.partial(accel_search, tm_count, chan_count), out...  1.1 us

profile of v6, /device:TPU:0, one launch (start us, length us, event | category | flops | bytes accessed | tf_op | source)
XLA Modules:
  0.0 17.6 jit_solution(1594871532414155164)
XLA Ops:
  0.0 0.0 copy-start
  0.0 2.0 %partial_series.1 = bf16[256,128]{1,0:T(8,128)(2,1)S(1)} custom-call(bf16[128,256]{1,0:T(8,128)(2,1)} %samples_hbm.1, s32[8,128]{1,0:T(8,128)} %bitcast.7, s32[1,32]{1,0:T(1,128)} %bitcast.8), custom_call_target="tpu_custom_call" | custom-call | tf_op jit(solution)/shard_map/partial_series/pallas_call | solution.py:239
  2.0 0.0 copy-start.1
  2.0 0.0 copy-start.2
  2.1 14.4 %all_to_all.11 = bf16[32,8,128]{2,1,0:T(8,128)(2,1)S(1)} all-to-all(bf16[32,8,128]{2,1,0:T(8,128)(2,1)S(1)} %bitcast.6), channel_id=1, replica_groups=mesh['tm'=4,'chan'=8] {'tm','chan'}, dimensions={0} | all-to-all | bytes 131072 | tf_op jit(solution)/shard_map/all_to_all | solution.py:265
  16.4 0.0 copy-done
  16.4 0.0 copy-done.1
  16.4 0.0 copy-done.2
  16.5 1.1 %accel_search.1 = bf16[128,128]{1,0:T(8,128)(2,1)} custom-call(bf16[256,128]{1,0:T(8,128)(2,1)S(1)} %bitcast.5, bf16[128,256]{1,0:T(8,128)(2,1)S(1)} %copy-done.1, bf16[256,256]{1,0:T(8,128)(2,1)S(1)} %copy-done, bf16[2,32,256]{2,1,0:T(8,128)(2,1)S(1)} %copy-done.2), custom_call_target="tpu_custom_call" | custom-call | tf_op jit(solution)/shard_map/accel_search/pallas_call | solution.py:267
Async XLA Ops:
  0.0 16.4 %copy-start = (bf16[256,256]{1,0:T(8,128)(2,1)S(1)}, bf16[256,256]{1,0:T(8,128)(2,1)}, u32[]{:S(2)}) copy-start(bf16[256,256]{1,0:T(8,128)(2,1)} %constant.4.clone.reverse_ref) | copy-start | bytes 393220
  2.0 14.4 %copy-start.1 = (bf16[128,256]{1,0:T(8,128)(2,1)S(1)}, bf16[128,256]{1,0:T(8,128)(2,1)}, u32[]{:S(2)}) copy-start(bf16[128,256]{1,0:T(8,128)(2,1)} %constant.5.clone.table_ref) | copy-start | bytes 196612
  2.0 14.4 %copy-start.2 = (bf16[2,32,256]{2,1,0:T(8,128)(2,1)S(1)}, bf16[2,32,256]{2,1,0:T(8,128)(2,1)}, u32[]{:S(2)}) copy-start(bf16[2,32,256]{2,1,0:T(8,128)(2,1)} %kernels_ref.1) | copy-start | bytes 98308

commit v7 on v6

--- a/solution.py
+++ b/solution.py
@@ -38,19 +38,29 @@
 
 def trial_blocks(value, chan_count):
     parts = []
-    for owner in range(chan_count):
+    for owner in reversed(range(chan_count)):
         rows = value[owner * TRIAL_DEV : (owner + 1) * TRIAL_DEV]
         parts += [rows[:, :LANES], rows[:, LANES:]]
-    return jnp.concatenate(parts, axis=0).astype(jnp.bfloat16)
+    return jnp.concatenate(parts, axis=0)
+
+
+def group_order(tm_count, chan_count):
+    groups = []
+    for odd in range(1, tm_count, 2):
+        for_both = sorted((odd, (odd + 1) % tm_count), reverse=True)
+        groups.append(
+            [block * chan_count + owner for block in for_both for owner in reversed(range(chan_count))]
+        )
+    return groups
 
 
 def partial_series(
-    tm_count,
     chan_count,
     samples_hbm,
     delay_hbm,
     tail_hbm,
-    out_ref,
+    late_ref,
+    early_ref,
     samples_ref,
     delay_ref,
     tail_ref,
@@ -74,7 +84,6 @@
     ]
     for copy in copies:
         copy.start()
-    out_ref[...] = jnp.zeros_like(out_ref)
     copies[0].wait()
     copies[1].wait()
 
@@ -161,29 +170,17 @@
     positions = lax.broadcasted_iota(jnp.int32, (trials, block_len), 1)
     late = (series[:, block_len:] + top_bin) * scale
     kept = positions.astype(jnp.float32) >= block_len - as_column(tails[:, :trials])
-    group = lax.axis_index("tm")
-    kept = jnp.logical_and(kept, group > 0)
     early = jnp.where(kept, series[:, :block_len] + top_bin + whole_block, 0.0) * scale
-
-    group_rows = chan_count * ROWS
-    before = lax.rem(group + tm_count - 1, tm_count)
-    for target, value in ((group, late), (before, early))[: min(tm_count, 2)]:
-        first = pl.multiple_of(target * group_rows, group_rows)
-        out_ref[pl.ds(first, group_rows), :] = trial_blocks(value, chan_count)
+    late_ref[...] = trial_blocks(late, chan_count)
+    early_ref[...] = trial_blocks(early, chan_count).astype(jnp.bfloat16)
 
 
 def accel_search(
-    tm_count, chan_count, parts_ref, table_ref, reverse_ref, kernels_ref, out_ref, windows, by_kernel
+    parts_ref, table_ref, reverse_ref, kernels_ref, out_ref, windows, by_kernel
 ):
-    group_rows = chan_count * ROWS
-    group = lax.axis_index("tm")
-    after = lax.rem(group + 1, tm_count)
-    own = parts_ref[pl.ds(pl.multiple_of(group * group_rows, group_rows), group_rows), :]
-    both = own.astype(jnp.float32)
-    if tm_count > 1:
-        following = parts_ref[pl.ds(pl.multiple_of(after * group_rows, group_rows), group_rows), :]
-        both += following.astype(jnp.float32)
-    series = jnp.sum(both.reshape(chan_count, ROWS, LANES), axis=0).astype(jnp.bfloat16)
+    sources = parts_ref.shape[0] // ROWS
+    parts = parts_ref[...].astype(jnp.float32).reshape(sources, ROWS, LANES)
+    series = jnp.sum(parts, axis=0).astype(jnp.bfloat16)
 
     half_len = LANES
     block_len = 2 * half_len
@@ -233,12 +230,15 @@
     channels, block_len = filterbank.shape
     trials = tail_len.shape[0]
     accels = kernels.shape[1]
-    devices = tm_count * chan_count
     total_rows = block_len + block_len // max(1, LANES // trials)
     total_rows = -(-total_rows // LANES) * LANES
-    parts = pl.pallas_call(
-        functools.partial(partial_series, tm_count, chan_count),
-        out_shape=jax.ShapeDtypeStruct((devices * ROWS, LANES), jnp.bfloat16),
+    group_rows = chan_count * ROWS
+    late, early = pl.pallas_call(
+        functools.partial(partial_series, chan_count),
+        out_shape=(
+            jax.ShapeDtypeStruct((group_rows, LANES), jnp.float32),
+            jax.ShapeDtypeStruct((group_rows, LANES), jnp.bfloat16),
+        ),
         in_specs=[pl.BlockSpec(memory_space=pltpu.HBM)] * 3,
         scratch_shapes=[
             pltpu.VMEM((channels, block_len), jnp.bfloat16),
@@ -262,10 +262,26 @@
             )
         )
     )
-    parts = lax.all_to_all(parts, ("tm", "chan"), 0, 0, tiled=True)
+    block = lax.axis_index("tm")
+    is_even = block % 2 == 0
+    tails = lax.ppermute(early, "tm", [(index, index ^ 1) for index in range(tm_count)])
+    own = (late + jnp.where(is_even, tails.astype(jnp.float32), 0.0)).astype(jnp.bfloat16)
+    other = jnp.where(jnp.logical_and(is_even, block > 0), early, jnp.zeros_like(early))
+    own_first = jnp.where(is_even, block > 0, block == tm_count - 1)
+    parts = jnp.concatenate(
+        [jnp.where(own_first, own, other), jnp.where(own_first, other, own)], axis=0
+    )
+    parts = lax.all_to_all(
+        parts,
+        ("tm", "chan"),
+        0,
+        0,
+        axis_index_groups=group_order(tm_count, chan_count),
+        tiled=True,
+    )
     reverse = jnp.asarray(np.eye(block_len, dtype=np.float32)[::-1], jnp.bfloat16)
     power = pl.pallas_call(
-        functools.partial(accel_search, tm_count, chan_count),
+        accel_search,
         out_shape=jax.ShapeDtypeStruct((accels * TRIAL_DEV, block_len // 2), jnp.bfloat16),
         scratch_shapes=[
             pltpu.VMEM((2 * block_len, TRIAL_DEV * block_len // 2), jnp.bfloat16),

time: 17.7 us -> 16.5 us (0.932)
  blocking collectives: 14.4 us -> 11.8 us
  waiting for transfers between devices: 0 us -> 0.84 us
  starting transfers between devices: 0 us -> 0.52 us
    all_to_all x1, blocking collectives: 14.4 us -> 11.8 us  [shards(): lax.all_to_all(parts, ('tm', 'chan'), 0, 0, axis_index_groups=group_order...]
    ppermute x0 -> x1, waiting for transfers between devices: none -> 0.84 us  [shards(): lax.ppermute(early, 'tm', [(index, index ^ 1) for index in range(tm_count)])]
    ppermute x0 -> x1, starting transfers between devices: none -> 0.52 us  [shards(): lax.ppermute(early, 'tm', [(index, index ^ 1) for index in range(tm_count)])]
  transfers between devices with their start and end apart: 0 -> 1, of which waited for: 0 -> 1; matrix products, arithmetic and copies ran while one was open for 0% -> 0% of each run, Pallas kernels for 0% -> 0%
where the time goes in v7:
time: 16.5 us; the launch traced here: 16.3 us
  blocking collectives  11.8 us (72%)
  Pallas kernels  3.09 us (19%)
  waiting for transfers between devices  0.84 us (5%)
  starting transfers between devices  0.52 us (3%)
    all_to_all x1, blocking collectives, shards(): lax.all_to_all(parts, ('tm', 'chan'), 0, 0, axis_index_groups=group_order...  11.8 us
    pallas_call x1, Pallas kernels, shards(): pl.pallas_call(functools.partial(partial_series, chan_count), out_shape=(...  1.99 us
    pallas_call x1, Pallas kernels, shards(): pl.pallas_call(accel_search, out_shape=jax.ShapeDtypeStruct((accels * TRI...  1.1 us
    ppermute x1, waiting for transfers between devices, shards(): lax.ppermute(early, 'tm', [(index, index ^ 1) for index in range(tm_count)])  0.84 us
    ppermute x1, starting transfers between devices, shards(): lax.ppermute(early, 'tm', [(index, index ^ 1) for index in range(tm_count)])  0.52 us
  transfers between devices with their start and end apart: 1, of which 1 were waited for; matrix products, arithmetic and copies ran while one was open for 0% of the time, Pallas kernels for 0%

profile of v7, /device:TPU:0, one launch (start us, length us, event | category | flops | bytes accessed | tf_op | source)
XLA Modules:
  0.0 16.3 jit_solution(12221032546766126196)
XLA Ops:
  0.0 2.0 %partial_series.1 = (f32[64,128]{1,0:T(8,128)S(1)}, bf16[64,128]{1,0:T(8,128)(2,1)S(1)}) custom-call(bf16[128,256]{1,0:T(8,128)(2,1)} %samples_hbm.1, s32[8,128]{1,0:T(8,128)} %bitcast.7, s32[1,32]{1,0:T(1,128)} %bitcast.8), custom_call_target="tpu_custom_call" | custom-call | tf_op jit(solution)/shard_map/partial_series/pallas_call | solution.py:236
  2.0 0.5 %collective-permute-start = (bf16[64,128]{1,0:T(8,128)(2,1)S(1)}, bf16[64,128]{1,0:T(8,128)(2,1)S(1)}, u32[]{:S(2)}, u32[]{:S(2)}) collective-permute-start(bf16[64,128]{1,0:T(8,128)(2,1)S(1)} %get-tuple-element.8), channel_id=1, source_target_pairs={{0,8},{8,0},{16,24},{24,16},{1,9},{9,1},{17,25},{25,17},{2,10},{10... | collective-permute-start | bytes 49160 | tf_op jit(solution)/shard_map/ppermute | solution.py:267
  2.5 0.8 %collective-permute-done = bf16[64,128]{1,0:T(8,128)(2,1)S(1)} collective-permute-done((bf16[64,128]{1,0:T(8,128)(2,1)S(1)}, bf16[64,128]{1,0:T(8,128)(2,1)S(1)}, u32[]{:S(2)}, u32[]{:S(2)}) %collective-permute-start) | collective-permute-done | bytes 16416 | tf_op jit(solution)/shard_map/ppermute | solution.py:267
  3.4 0.0 copy-start
  3.4 0.0 copy-start.1
  3.4 0.0 copy-start.2
  3.4 11.8 %all_to_all.11 = bf16[16,8,128]{2,1,0:T(8,128)(2,1)S(1)} all-to-all(bf16[16,8,128]{2,1,0:T(8,128)(2,1)S(1)} %maximum_bitcast_fusion), channel_id=1, replica_groups={{23,22,21,20,19,18,17,16,15,14,13,12,11,10,9,8},{31,30,29,28,27,26,25,2..., dimensions={0} | all-to-all | bytes 65536 | tf_op jit(solution)/shard_map/all_to_all | solution.py:274
  15.2 0.0 copy-done
  15.2 0.0 copy-done.1
  15.2 0.0 copy-done.2
  15.2 1.1 %accel_search.1 = bf16[128,128]{1,0:T(8,128)(2,1)} custom-call(bf16[128,128]{1,0:T(8,128)(2,1)S(1)} %bitcast.6, bf16[128,256]{1,0:T(8,128)(2,1)S(1)} %copy-done.1, bf16[256,256]{1,0:T(8,128)(2,1)S(1)} %copy-done, bf16[2,32,256]{2,1,0:T(8,128)(2,1)S(1)} %copy-done.2), custom_call_target="tpu_custom_call" | custom-call | tf_op jit(solution)/shard_map/accel_search/pallas_call | solution.py:283
  (3 shorter events, 0.0 us)
Async XLA Ops:
  2.0 1.4 %collective-permute-start = (bf16[64,128]{1,0:T(8,128)(2,1)S(1)}, bf16[64,128]{1,0:T(8,128)(2,1)S(1)}, u32[]{:S(2)}, u32[]{:S(2)}) collective-permute-start(bf16[64,128]{1,0:T(8,128)(2,1)S(1)} %get-tuple-element.8), channel_id=1, source_target_pairs={{0,8},{8,0},{16,24},{24,16},{1,9},{9,1},{17,25},{25,17},{2,10},{10... | collective-permute-start | bytes 49160 | tf_op jit(solution)/shard_map/ppermute | solution.py:267
  3.4 11.8 %copy-start = (bf16[256,256]{1,0:T(8,128)(2,1)S(1)}, bf16[256,256]{1,0:T(8,128)(2,1)}, u32[]{:S(2)}) copy-start(bf16[256,256]{1,0:T(8,128)(2,1)} %constant.29.clone.reverse_ref) | copy-start | bytes 393220
  3.4 11.8 %copy-start.1 = (bf16[128,256]{1,0:T(8,128)(2,1)S(1)}, bf16[128,256]{1,0:T(8,128)(2,1)}, u32[]{:S(2)}) copy-start(bf16[128,256]{1,0:T(8,128)(2,1)} %constant.30.clone.table_ref) | copy-start | bytes 196612
  3.4 11.8 %copy-start.2 = (bf16[2,32,256]{2,1,0:T(8,128)(2,1)S(1)}, bf16[2,32,256]{2,1,0:T(8,128)(2,1)}, u32[]{:S(2)}) copy-start(bf16[2,32,256]{2,1,0:T(8,128)(2,1)} %kernels_ref.1) | copy-start | bytes 98308

commit v8 on v7

--- a/solution.py
+++ b/solution.py
@@ -36,9 +36,13 @@
     return jnp.sum(jnp.where(rows == columns, row, 0.0), axis=1, keepdims=True)
 
 
+def chan_order(chan_count):
+    return [chan_count - 1] + list(range(chan_count - 1))
+
+
 def trial_blocks(value, chan_count):
     parts = []
-    for owner in reversed(range(chan_count)):
+    for owner in chan_order(chan_count):
         rows = value[owner * TRIAL_DEV : (owner + 1) * TRIAL_DEV]
         parts += [rows[:, :LANES], rows[:, LANES:]]
     return jnp.concatenate(parts, axis=0)
@@ -47,9 +51,9 @@
 def group_order(tm_count, chan_count):
     groups = []
     for odd in range(1, tm_count, 2):
-        for_both = sorted((odd, (odd + 1) % tm_count), reverse=True)
+        blocks = sorted((odd, (odd + 1) % tm_count))
         groups.append(
-            [block * chan_count + owner for block in for_both for owner in reversed(range(chan_count))]
+            [block * chan_count + owner for block in blocks for owner in chan_order(chan_count)]
         )
     return groups
 
@@ -267,7 +271,7 @@
     tails = lax.ppermute(early, "tm", [(index, index ^ 1) for index in range(tm_count)])
     own = (late + jnp.where(is_even, tails.astype(jnp.float32), 0.0)).astype(jnp.bfloat16)
     other = jnp.where(jnp.logical_and(is_even, block > 0), early, jnp.zeros_like(early))
-    own_first = jnp.where(is_even, block > 0, block == tm_count - 1)
+    own_first = jnp.where(is_even, block == 0, block < tm_count - 1)
     parts = jnp.concatenate(
         [jnp.where(own_first, own, other), jnp.where(own_first, other, own)], axis=0
     )

time: 16.5 us -> 16.1 us (0.976)
  blocking collectives: 11.8 us -> 11.4 us
    all_to_all x1, blocking collectives: 11.8 us -> 11.4 us  [shards(): lax.all_to_all(parts, ('tm', 'chan'), 0, 0, axis_index_groups=group_order...]
where the time goes in v8:
time: 16.1 us; the launch traced here: 15.9 us
  blocking collectives  11.4 us (71%)
  Pallas kernels  3.09 us (19%)
  waiting for transfers between devices  0.84 us (5%)
  starting transfers between devices  0.52 us (3%)
    all_to_all x1, blocking collectives, shards(): lax.all_to_all(parts, ('tm', 'chan'), 0, 0, axis_index_groups=group_order...  11.4 us
    pallas_call x1, Pallas kernels, shards(): pl.pallas_call(functools.partial(partial_series, chan_count), out_shape=(...  1.99 us
    pallas_call x1, Pallas kernels, shards(): pl.pallas_call(accel_search, out_shape=jax.ShapeDtypeStruct((accels * TRI...  1.1 us
    ppermute x1, waiting for transfers between devices, shards(): lax.ppermute(early, 'tm', [(index, index ^ 1) for index in range(tm_count)])  0.84 us
    ppermute x1, starting transfers between devices, shards(): lax.ppermute(early, 'tm', [(index, index ^ 1) for index in range(tm_count)])  0.52 us
  transfers between devices with their start and end apart: 1, of which 1 were waited for; matrix products, arithmetic and copies ran while one was open for 0% of the time, Pallas kernels for 0%

profile of v8, /device:TPU:0, one launch (start us, length us, event | category | flops | bytes accessed | tf_op | source)
XLA Modules:
  0.0 15.9 jit_solution(312329754106378534)
XLA Ops:
  0.0 2.0 %partial_series.1 = (f32[64,128]{1,0:T(8,128)S(1)}, bf16[64,128]{1,0:T(8,128)(2,1)S(1)}) custom-call(bf16[128,256]{1,0:T(8,128)(2,1)} %samples_hbm.1, s32[8,128]{1,0:T(8,128)} %bitcast.7, s32[1,32]{1,0:T(1,128)} %bitcast.8), custom_call_target="tpu_custom_call" | custom-call | tf_op jit(solution)/shard_map/partial_series/pallas_call | solution.py:240
  2.0 0.5 %collective-permute-start = (bf16[64,128]{1,0:T(8,128)(2,1)S(1)}, bf16[64,128]{1,0:T(8,128)(2,1)S(1)}, u32[]{:S(2)}, u32[]{:S(2)}) collective-permute-start(bf16[64,128]{1,0:T(8,128)(2,1)S(1)} %get-tuple-element.8), channel_id=1, source_target_pairs={{0,8},{8,0},{16,24},{24,16},{1,9},{9,1},{17,25},{25,17},{2,10},{10... | collective-permute-start | bytes 49160 | tf_op jit(solution)/shard_map/ppermute | solution.py:271
  2.5 0.8 %collective-permute-done = bf16[64,128]{1,0:T(8,128)(2,1)S(1)} collective-permute-done((bf16[64,128]{1,0:T(8,128)(2,1)S(1)}, bf16[64,128]{1,0:T(8,128)(2,1)S(1)}, u32[]{:S(2)}, u32[]{:S(2)}) %collective-permute-start) | collective-permute-done | bytes 16416 | tf_op jit(solution)/shard_map/ppermute | solution.py:271
  3.4 0.0 copy-start
  3.4 0.0 copy-start.1
  3.4 0.0 copy-start.2
  3.4 11.4 %all_to_all.11 = bf16[16,8,128]{2,1,0:T(8,128)(2,1)S(1)} all-to-all(bf16[16,8,128]{2,1,0:T(8,128)(2,1)S(1)} %maximum_bitcast_fusion), channel_id=1, replica_groups={{15,8,9,10,11,12,13,14,23,16,17,18,19,20,21,22},{7,0,1,2,3,4,5,6,31,24,..., dimensions={0} | all-to-all | bytes 65536 | tf_op jit(solution)/shard_map/all_to_all | solution.py:278
  14.8 0.0 copy-done
  14.8 0.0 copy-done.1
  14.8 0.0 copy-done.2
  14.8 1.1 %accel_search.1 = bf16[128,128]{1,0:T(8,128)(2,1)} custom-call(bf16[128,128]{1,0:T(8,128)(2,1)S(1)} %bitcast.6, bf16[128,256]{1,0:T(8,128)(2,1)S(1)} %copy-done.1, bf16[256,256]{1,0:T(8,128)(2,1)S(1)} %copy-done, bf16[2,32,256]{2,1,0:T(8,128)(2,1)S(1)} %copy-done.2), custom_call_target="tpu_custom_call" | custom-call | tf_op jit(solution)/shard_map/accel_search/pallas_call | solution.py:287
  (3 shorter events, 0.0 us)
Async XLA Ops:
  2.0 1.4 %collective-permute-start = (bf16[64,128]{1,0:T(8,128)(2,1)S(1)}, bf16[64,128]{1,0:T(8,128)(2,1)S(1)}, u32[]{:S(2)}, u32[]{:S(2)}) collective-permute-start(bf16[64,128]{1,0:T(8,128)(2,1)S(1)} %get-tuple-element.8), channel_id=1, source_target_pairs={{0,8},{8,0},{16,24},{24,16},{1,9},{9,1},{17,25},{25,17},{2,10},{10... | collective-permute-start | bytes 49160 | tf_op jit(solution)/shard_map/ppermute | solution.py:271
  3.4 11.5 %copy-start = (bf16[256,256]{1,0:T(8,128)(2,1)S(1)}, bf16[256,256]{1,0:T(8,128)(2,1)}, u32[]{:S(2)}) copy-start(bf16[256,256]{1,0:T(8,128)(2,1)} %constant.29.clone.reverse_ref) | copy-start | bytes 393220
  3.4 11.4 %copy-start.1 = (bf16[128,256]{1,0:T(8,128)(2,1)S(1)}, bf16[128,256]{1,0:T(8,128)(2,1)}, u32[]{:S(2)}) copy-start(bf16[128,256]{1,0:T(8,128)(2,1)} %constant.30.clone.table_ref) | copy-start | bytes 196612
  3.4 11.4 %copy-start.2 = (bf16[2,32,256]{2,1,0:T(8,128)(2,1)S(1)}, bf16[2,32,256]{2,1,0:T(8,128)(2,1)}, u32[]{:S(2)}) copy-start(bf16[2,32,256]{2,1,0:T(8,128)(2,1)} %kernels_ref.1) | copy-start | bytes 98308

commit v9 on v8

--- a/solution.py
+++ b/solution.py
@@ -58,19 +58,31 @@
     return groups
 
 
+def fold(total, trials, block_len):
+    width = total.shape[1]
+    repeats = width // trials
+    repeat_of = lax.broadcasted_iota(jnp.int32, (block_len, width), 1) // trials
+    sums = total[:block_len]
+    for repeat in range(1, repeats):
+        first = repeat * STEP
+        sums = jnp.where(repeat_of == repeat, total[first : first + block_len], sums)
+    turned_back = sums.T
+    return sum(turned_back[repeat * trials : (repeat + 1) * trials] for repeat in range(repeats))
+
+
 def partial_series(
     chan_count,
     samples_hbm,
     delay_hbm,
     tail_hbm,
-    late_ref,
     early_ref,
+    moved,
+    chosen,
+    top_bin_ref,
     samples_ref,
     delay_ref,
     tail_ref,
     turned,
-    moved,
-    chosen,
     total,
     arrived,
 ):
@@ -96,7 +108,7 @@
     shifts = jnp.floor(delays * tails * (1.0 / MAXDELAY))
     columns = lax.broadcasted_iota(jnp.int32, (channels, width), 1)
     repeat_of = columns // trials
-    rests = (shifts - STEP * groups * repeat_of.astype(jnp.float32)).astype(jnp.bfloat16)
+    rests = (shifts - STEP * repeat_of.astype(jnp.float32)).astype(jnp.bfloat16)
     one = jnp.ones((), jnp.bfloat16)
     zero = jnp.zeros((), jnp.bfloat16)
 
@@ -108,7 +120,7 @@
             for group in range(first, min(first + pair, groups)):
                 chosen[
                     fine * channels : (fine + 1) * channels, group * width : (group + 1) * width
-                ] = where_rest_is(STEP * group + fine)
+                ] = where_rest_is(STEP * repeats * group + fine)
 
     own_shifts = shifts[:, :trials]
     whole = jnp.where(own_shifts == block_len, one, zero)
@@ -123,25 +135,22 @@
         moved[:, fine * channels : (fine + 1) * channels] = turned[fine : fine + rows].astype(
             jnp.bfloat16
         )
-    filled = STEP * (groups - 1)
-    total[:filled] = jnp.zeros((filled, width), jnp.float32)
-    rest = total.shape[0] - filled - block_len - STEP
-    if rest:
-        total[filled + block_len + STEP :] = jnp.zeros((rest, width), jnp.float32)
-    for first in range(0, groups, pair):
+    step = STEP * repeats
+    end = block_len + step - STEP
+    total[...] = jnp.zeros_like(total)
+    firsts = list(range(0, groups, pair))
+    half = len(firsts) // 2
+    for first in firsts[half:][::-1] + firsts[:half]:
         choose(first)
         last = min(first + pair, groups)
         sums = jnp.dot(
-            moved[...], chosen[:, first * width : last * width], preferred_element_type=jnp.float32
+            moved[: step * last],
+            chosen[:, first * width : last * width],
+            preferred_element_type=jnp.float32,
         )
         for group in range(first, last):
-            start = STEP * (groups - 1 - group)
             columns_of = slice((group - first) * width, (group - first + 1) * width)
-            rows_of = slice(start, start + block_len + STEP)
-            if group == 0:
-                total[rows_of] = sums[: block_len + STEP, columns_of]
-            else:
-                total[rows_of] += sums[: block_len + STEP, columns_of]
+            total[end - step * (group + 1) : end] += sums[: step * (group + 1), columns_of]
     signs = lax.broadcasted_iota(jnp.int32, (block_len, block_len), 0)
     signs += lax.broadcasted_iota(jnp.int32, (block_len, block_len), 1)
     nyquist_step = 0.5 / block_len
@@ -155,32 +164,38 @@
     whole_block = lax.dot_general(
         whole, samples, over_channels, preferred_element_type=jnp.float32
     )
-    turned_back = total[...].T
-    sums_by_rest = {}
-    for repeat in range(repeats):
-        part = turned_back[repeat * trials : (repeat + 1) * trials]
-        offset = block_len - STEP * groups * (repeat + 1)
-        before = offset // LANES * LANES
-        after = 2 * block_len - before - part.shape[1]
-        if before:
-            part = jnp.concatenate([jnp.zeros((trials, before), jnp.float32), part], axis=1)
-        if after > 0:
-            part = jnp.concatenate([part, jnp.zeros((trials, after), jnp.float32)], axis=1)
-        part = part[:, : 2 * block_len]
-        rest = offset - before
-        sums_by_rest[rest] = sums_by_rest[rest] + part if rest in sums_by_rest else part
-    series = sum(pltpu.roll(part, rest, 1) if rest else part for rest, part in sums_by_rest.items())
-    scale = 1.0 / math.sqrt(channels * chan_count)
+    early = fold(total, trials, block_len) + top_bin + whole_block
     positions = lax.broadcasted_iota(jnp.int32, (trials, block_len), 1)
-    late = (series[:, block_len:] + top_bin) * scale
     kept = positions.astype(jnp.float32) >= block_len - as_column(tails[:, :trials])
-    early = jnp.where(kept, series[:, :block_len] + top_bin + whole_block, 0.0) * scale
+    early = jnp.where(kept, early, 0.0) * (1.0 / math.sqrt(channels * chan_count))
+    early_ref[...] = trial_blocks(early, chan_count).astype(jnp.bfloat16)
+    top_bin_ref[...] = top_bin
+
+
+def late_series(chan_count, scale, moved, chosen, top_bin_ref, late_ref, total):
+    trials, block_len = top_bin_ref.shape
+    repeats = max(1, LANES // trials)
+    width = repeats * trials
+    step = STEP * repeats
+    groups = block_len // step
+    pair = max(1, 2 * LANES // width)
+    total[...] = jnp.zeros_like(total)
+    for first in range(0, groups, pair):
+        last = min(first + pair, groups)
+        start = step * first
+        sums = jnp.dot(
+            moved[start:], chosen[:, first * width : last * width], preferred_element_type=jnp.float32
+        )
+        for group in range(first, last):
+            columns_of = slice((group - first) * width, (group - first + 1) * width)
+            rows_of = slice(step * group + STEP - start, block_len + STEP - start)
+            total[: block_len - step * group] += sums[rows_of, columns_of]
+    late = (fold(total, trials, block_len) + top_bin_ref[...]) * scale
     late_ref[...] = trial_blocks(late, chan_count)
-    early_ref[...] = trial_blocks(early, chan_count).astype(jnp.bfloat16)
 
 
 def accel_search(
-    parts_ref, table_ref, reverse_ref, kernels_ref, out_ref, windows, by_kernel
+    parts_ref, table_ref, kernels_ref, out_ref, windows, by_kernel
 ):
     sources = parts_ref.shape[0] // ROWS
     parts = parts_ref[...].astype(jnp.float32).reshape(sources, ROWS, LANES)
@@ -211,8 +226,11 @@
                 early, zero, turned
             )
 
+    ends = lax.broadcasted_iota(jnp.int32, (block_len, block_len), 0)
+    ends += lax.broadcasted_iota(jnp.int32, (block_len, block_len), 1)
+    reverse = jnp.where(ends == block_len - 1, 1.0, 0.0).astype(jnp.bfloat16)
     real, imag = (
-        jnp.dot(kernels_ref[part], reverse_ref[...], preferred_element_type=jnp.float32).astype(
+        jnp.dot(kernels_ref[part], reverse, preferred_element_type=jnp.float32).astype(
             jnp.bfloat16
         )
         for part in range(2)
@@ -234,14 +252,16 @@
     channels, block_len = filterbank.shape
     trials = tail_len.shape[0]
     accels = kernels.shape[1]
-    total_rows = block_len + block_len // max(1, LANES // trials)
-    total_rows = -(-total_rows // LANES) * LANES
+    total_rows = block_len + STEP * (max(1, LANES // trials) - 1)
+    total = pltpu.VMEM((total_rows, max(LANES, trials)), jnp.float32)
     group_rows = chan_count * ROWS
-    late, early = pl.pallas_call(
+    early, moved, chosen, top_bin = pl.pallas_call(
         functools.partial(partial_series, chan_count),
         out_shape=(
-            jax.ShapeDtypeStruct((group_rows, LANES), jnp.float32),
             jax.ShapeDtypeStruct((group_rows, LANES), jnp.bfloat16),
+            jax.ShapeDtypeStruct((block_len + 2 * STEP, STEP * channels), jnp.bfloat16),
+            jax.ShapeDtypeStruct((STEP * channels, block_len // STEP * trials), jnp.bfloat16),
+            jax.ShapeDtypeStruct((trials, block_len), jnp.float32),
         ),
         in_specs=[pl.BlockSpec(memory_space=pltpu.HBM)] * 3,
         scratch_shapes=[
@@ -249,9 +269,7 @@
             pltpu.VMEM((chan_count, channels), jnp.int32),
             pltpu.VMEM((1, trials), jnp.int32),
             pltpu.VMEM((block_len + 3 * STEP, channels), jnp.float32),
-            pltpu.VMEM((block_len + 2 * STEP, STEP * channels), jnp.bfloat16),
-            pltpu.VMEM((STEP * channels, block_len // STEP * trials), jnp.bfloat16),
-            pltpu.VMEM((total_rows, max(LANES, trials)), jnp.float32),
+            total,
             pltpu.SemaphoreType.DMA((3,)),
         ],
         compiler_params=pltpu.CompilerParams(vmem_limit_bytes=40 * 1024 * 1024),
@@ -266,9 +284,21 @@
             )
         )
     )
+    tails = lax.ppermute(early, "tm", [(index, index ^ 1) for index in range(tm_count)])
+    late = pl.pallas_call(
+        functools.partial(late_series, chan_count, 1.0 / math.sqrt(channels * chan_count)),
+        out_shape=jax.ShapeDtypeStruct((group_rows, LANES), jnp.float32),
+        scratch_shapes=[total],
+        compiler_params=pltpu.CompilerParams(vmem_limit_bytes=16 * 1024 * 1024),
+        cost_estimate=pl.CostEstimate(
+            flops=2 * block_len * STEP * channels * block_len // STEP * trials,
+            bytes_accessed=4 * block_len * block_len,
+            transcendentals=0,
+        ),
+        name="late_series",
+    )(moved, chosen, top_bin)
     block = lax.axis_index("tm")
     is_even = block % 2 == 0
-    tails = lax.ppermute(early, "tm", [(index, index ^ 1) for index in range(tm_count)])
     own = (late + jnp.where(is_even, tails.astype(jnp.float32), 0.0)).astype(jnp.bfloat16)
     other = jnp.where(jnp.logical_and(is_even, block > 0), early, jnp.zeros_like(early))
     own_first = jnp.where(is_even, block == 0, block < tm_count - 1)
@@ -283,7 +313,6 @@
         axis_index_groups=group_order(tm_count, chan_count),
         tiled=True,
     )
-    reverse = jnp.asarray(np.eye(block_len, dtype=np.float32)[::-1], jnp.bfloat16)
     power = pl.pallas_call(
         accel_search,
         out_shape=jax.ShapeDtypeStruct((accels * TRIAL_DEV, block_len // 2), jnp.bfloat16),
@@ -293,7 +322,7 @@
         ],
         compiler_params=pltpu.CompilerParams(vmem_limit_bytes=40 * 1024 * 1024),
         name="accel_search",
-    )(parts, bin_table(block_len), reverse, kernels)
+    )(parts, bin_table(block_len), kernels)
     return power.reshape(accels, TRIAL_DEV, block_len // 2)
 
 

time: 16.1 us -> 15.9 us (0.988)
  waiting for transfers between devices: 0.84 us -> 0.14 us
  Pallas kernels: 3.09 us -> 3.73 us
    ppermute x1, waiting for transfers between devices: 0.84 us -> 0.14 us  [shards(): lax.ppermute(early, 'tm', [(index, index ^ 1) for index in range(tm_count)])]
    pallas_call x0 -> x1, Pallas kernels: none -> 0.67 us  [shards(): pl.pallas_call(functools.partial(late_series, chan_count, 1.0 / math.sqrt...]
  transfers between devices with their start and end apart: 1 -> 1, of which waited for: 1 -> 1; matrix products, arithmetic and copies ran while one was open for 0% -> 0% of each run, Pallas kernels for 0% -> 4%
where the time goes in v9:
time: 15.9 us; the launch traced here: 15.8 us
  blocking collectives  11.3 us (71%)
  Pallas kernels  3.73 us (23%)
  starting transfers between devices  0.52 us (3%)
    all_to_all x1, blocking collectives, shards(): lax.all_to_all(parts, ('tm', 'chan'), 0, 0, axis_index_groups=group_order...  11.3 us
    pallas_call x1, Pallas kernels, shards(): pl.pallas_call(functools.partial(partial_series, chan_count), out_shape=(...  1.97 us
    pallas_call x1, Pallas kernels, shards(): pl.pallas_call(accel_search, out_shape=jax.ShapeDtypeStruct((accels * TRI...  1.1 us
    pallas_call x1, Pallas kernels, shards(): pl.pallas_call(functools.partial(late_series, chan_count, 1.0 / math.sqrt...  0.67 us
    ppermute x1, starting transfers between devices, shards(): lax.ppermute(early, 'tm', [(index, index ^ 1) for index in range(tm_count)])  0.52 us
  transfers between devices with their start and end apart: 1, of which 1 were waited for; matrix products, arithmetic and copies ran while one was open for 0% of the time, Pallas kernels for 4%

profile of v9, /device:TPU:0, one launch (start us, length us, event | category | flops | bytes accessed | tf_op | source)
XLA Modules:
  0.0 15.8 jit_solution(1541367727751280352)
XLA Ops:
  0.0 0.0 copy-start
  0.0 0.0 copy-start.1
  0.0 2.0 %partial_series.1 = (bf16[64,128]{1,0:T(8,128)(2,1)S(1)}, bf16[272,1024]{1,0:T(8,128)(2,1)S(1)}, bf16[1024,1024]{1,0:T(8,128)(2,1)S(1)}, f32[32,256]{1,0:T(8,128)S(1)}) custom-call(bf16[128,256]{1,0:T(8,128)(2,1)} %samples_hbm.1, s32[8,128]{1,0:T(8,128)} %bitcast.7, s32[1,32]{1,0:T(1,128)} %bitcast.8), custom_call_target="tpu_custom_call" | custom-call | tf_op jit(solution)/shard_map/partial_series/pallas_call | solution.py:258
  2.0 0.5 %collective-permute-start = (bf16[64,128]{1,0:T(8,128)(2,1)S(1)}, bf16[64,128]{1,0:T(8,128)(2,1)S(1)}, u32[]{:S(2)}, u32[]{:S(2)}) collective-permute-start(bf16[64,128]{1,0:T(8,128)(2,1)S(1)} %get-tuple-element.12), channel_id=1, source_target_pairs={{0,8},{8,0},{16,24},{24,16},{1,9},{9,1},{17,25},{25,17},{2,10},{10... | collective-permute-start | bytes 49160 | tf_op jit(solution)/shard_map/ppermute | solution.py:287
  2.5 0.7 %late_series.1 = f32[64,128]{1,0:T(8,128)S(1)} custom-call(bf16[272,1024]{1,0:T(8,128)(2,1)S(1)} %get-tuple-element.9.moved, bf16[1024,1024]{1,0:T(8,128)(2,1)S(1)} %get-tuple-element.10.chosen, f32[32,256]{1,0:T(8,128)S(1)} %get-tuple-element.11.top_bin_ref), custom_call_target="tpu_custom_call" | custom-call | flops 536870912 | bytes 262144 | tf_op jit(solution)/shard_map/late_series/pallas_call | solution.py:288
  3.2 0.1 collective-permute-done
  3.4 11.3 %all_to_all.11 = bf16[16,8,128]{2,1,0:T(8,128)(2,1)S(1)} all-to-all(bf16[16,8,128]{2,1,0:T(8,128)(2,1)S(1)} %maximum_bitcast_fusion), channel_id=1, replica_groups={{15,8,9,10,11,12,13,14,23,16,17,18,19,20,21,22},{7,0,1,2,3,4,5,6,31,24,..., dimensions={0} | all-to-all | bytes 65536 | tf_op jit(solution)/shard_map/all_to_all | solution.py:308
  14.6 0.0 copy-done
  14.7 0.0 copy-done.1
  14.7 1.1 %accel_search.1 = bf16[128,128]{1,0:T(8,128)(2,1)} custom-call(bf16[128,128]{1,0:T(8,128)(2,1)S(1)} %bitcast.6, bf16[128,256]{1,0:T(8,128)(2,1)S(1)} %copy-done, bf16[2,32,256]{2,1,0:T(8,128)(2,1)S(1)} %copy-done.1), custom_call_target="tpu_custom_call" | custom-call | tf_op jit(solution)/shard_map/accel_search/pallas_call | solution.py:316
  (3 shorter events, 0.0 us)
Async XLA Ops:
  0.0 14.6 %copy-start = (bf16[128,256]{1,0:T(8,128)(2,1)S(1)}, bf16[128,256]{1,0:T(8,128)(2,1)}, u32[]{:S(2)}) copy-start(bf16[128,256]{1,0:T(8,128)(2,1)} %constant.27.clone.table_ref) | copy-start | bytes 196612
  0.0 14.7 %copy-start.1 = (bf16[2,32,256]{2,1,0:T(8,128)(2,1)S(1)}, bf16[2,32,256]{2,1,0:T(8,128)(2,1)}, u32[]{:S(2)}) copy-start(bf16[2,32,256]{2,1,0:T(8,128)(2,1)} %kernels_ref.1) | copy-start | bytes 98308
  2.0 1.4 %collective-permute-start = (bf16[64,128]{1,0:T(8,128)(2,1)S(1)}, bf16[64,128]{1,0:T(8,128)(2,1)S(1)}, u32[]{:S(2)}, u32[]{:S(2)}) collective-permute-start(bf16[64,128]{1,0:T(8,128)(2,1)S(1)} %get-tuple-element.12), channel_id=1, source_target_pairs={{0,8},{8,0},{16,24},{24,16},{1,9},{9,1},{17,25},{25,17},{2,10},{10... | collective-permute-start | bytes 49160 | tf_op jit(solution)/shard_map/ppermute | solution.py:287

commit v10 on v9

--- a/solution.py
+++ b/solution.py
@@ -122,6 +122,11 @@
                     fine * channels : (fine + 1) * channels, group * width : (group + 1) * width
                 ] = where_rest_is(STEP * repeats * group + fine)
 
+    firsts = list(range(0, groups, pair))
+    half = len(firsts) // 2
+    firsts = firsts[half:][::-1] + firsts[:half]
+    for first in firsts[:1]:
+        choose(first)
     own_shifts = shifts[:, :trials]
     whole = jnp.where(own_shifts == block_len, one, zero)
     parity = jnp.where(own_shifts - 2.0 * jnp.floor(own_shifts * 0.5) == 0.0, one, -one)
@@ -138,10 +143,9 @@
     step = STEP * repeats
     end = block_len + step - STEP
     total[...] = jnp.zeros_like(total)
-    firsts = list(range(0, groups, pair))
-    half = len(firsts) // 2
-    for first in firsts[half:][::-1] + firsts[:half]:
-        choose(first)
+    for index, first in enumerate(firsts):
+        if index >= 1:
+            choose(first)
         last = min(first + pair, groups)
         sums = jnp.dot(
             moved[: step * last],

time: 15.9 us -> 15.8 us (level)
  no operation moved by 1% of the time
where the time goes in v10:
time: 15.8 us; the launch traced here: 15.7 us
  blocking collectives  11.3 us (72%)
  Pallas kernels  3.65 us (23%)
  starting transfers between devices  0.51 us (3%)
    all_to_all x1, blocking collectives, shards(): lax.all_to_all(parts, ('tm', 'chan'), 0, 0, axis_index_groups=group_order...  11.3 us
    pallas_call x1, Pallas kernels, shards(): pl.pallas_call(functools.partial(partial_series, chan_count), out_shape=(...  1.88 us
    pallas_call x1, Pallas kernels, shards(): pl.pallas_call(accel_search, out_shape=jax.ShapeDtypeStruct((accels * TRI...  1.09 us
    pallas_call x1, Pallas kernels, shards(): pl.pallas_call(functools.partial(late_series, chan_count, 1.0 / math.sqrt...  0.67 us
    ppermute x1, starting transfers between devices, shards(): lax.ppermute(early, 'tm', [(index, index ^ 1) for index in range(tm_count)])  0.51 us
  transfers between devices with their start and end apart: 1, of which 1 were waited for; matrix products, arithmetic and copies ran while one was open for 0% of the time, Pallas kernels for 4%

profile of v10, /device:TPU:0, one launch (start us, length us, event | category | flops | bytes accessed | tf_op | source)
XLA Modules:
  0.0 15.7 jit_solution(15210877336277255010)
XLA Ops:
  0.0 0.0 copy-start
  0.0 0.0 copy-start.1
  0.0 1.9 %partial_series.1 = (bf16[64,128]{1,0:T(8,128)(2,1)S(1)}, bf16[272,1024]{1,0:T(8,128)(2,1)S(1)}, bf16[1024,1024]{1,0:T(8,128)(2,1)S(1)}, f32[32,256]{1,0:T(8,128)S(1)}) custom-call(bf16[128,256]{1,0:T(8,128)(2,1)} %samples_hbm.1, s32[8,128]{1,0:T(8,128)} %bitcast.7, s32[1,32]{1,0:T(1,128)} %bitcast.8), custom_call_target="tpu_custom_call" | custom-call | tf_op jit(solution)/shard_map/partial_series/pallas_call | solution.py:262
  1.9 0.5 %collective-permute-start = (bf16[64,128]{1,0:T(8,128)(2,1)S(1)}, bf16[64,128]{1,0:T(8,128)(2,1)S(1)}, u32[]{:S(2)}, u32[]{:S(2)}) collective-permute-start(bf16[64,128]{1,0:T(8,128)(2,1)S(1)} %get-tuple-element.12), channel_id=1, source_target_pairs={{0,8},{8,0},{16,24},{24,16},{1,9},{9,1},{17,25},{25,17},{2,10},{10... | collective-permute-start | bytes 49160 | tf_op jit(solution)/shard_map/ppermute | solution.py:291
  2.4 0.7 %late_series.1 = f32[64,128]{1,0:T(8,128)S(1)} custom-call(bf16[272,1024]{1,0:T(8,128)(2,1)S(1)} %get-tuple-element.9.moved, bf16[1024,1024]{1,0:T(8,128)(2,1)S(1)} %get-tuple-element.10.chosen, f32[32,256]{1,0:T(8,128)S(1)} %get-tuple-element.11.top_bin_ref), custom_call_target="tpu_custom_call" | custom-call | flops 536870912 | bytes 262144 | tf_op jit(solution)/shard_map/late_series/pallas_call | solution.py:292
  3.1 0.1 collective-permute-done
  3.3 11.3 %all_to_all.11 = bf16[16,8,128]{2,1,0:T(8,128)(2,1)S(1)} all-to-all(bf16[16,8,128]{2,1,0:T(8,128)(2,1)S(1)} %maximum_bitcast_fusion), channel_id=1, replica_groups={{15,8,9,10,11,12,13,14,23,16,17,18,19,20,21,22},{7,0,1,2,3,4,5,6,31,24,..., dimensions={0} | all-to-all | bytes 65536 | tf_op jit(solution)/shard_map/all_to_all | solution.py:312
  14.6 0.0 copy-done
  14.6 0.0 copy-done.1
  14.6 1.1 %accel_search.1 = bf16[128,128]{1,0:T(8,128)(2,1)} custom-call(bf16[128,128]{1,0:T(8,128)(2,1)S(1)} %bitcast.6, bf16[128,256]{1,0:T(8,128)(2,1)S(1)} %copy-done, bf16[2,32,256]{2,1,0:T(8,128)(2,1)S(1)} %copy-done.1), custom_call_target="tpu_custom_call" | custom-call | tf_op jit(solution)/shard_map/accel_search/pallas_call | solution.py:320
  (3 shorter events, 0.0 us)
Async XLA Ops:
  0.0 14.6 %copy-start = (bf16[128,256]{1,0:T(8,128)(2,1)S(1)}, bf16[128,256]{1,0:T(8,128)(2,1)}, u32[]{:S(2)}) copy-start(bf16[128,256]{1,0:T(8,128)(2,1)} %constant.27.clone.table_ref) | copy-start | bytes 196612
  0.0 14.6 %copy-start.1 = (bf16[2,32,256]{2,1,0:T(8,128)(2,1)S(1)}, bf16[2,32,256]{2,1,0:T(8,128)(2,1)}, u32[]{:S(2)}) copy-start(bf16[2,32,256]{2,1,0:T(8,128)(2,1)} %kernels_ref.1) | copy-start | bytes 98308
  1.9 1.4 %collective-permute-start = (bf16[64,128]{1,0:T(8,128)(2,1)S(1)}, bf16[64,128]{1,0:T(8,128)(2,1)S(1)}, u32[]{:S(2)}, u32[]{:S(2)}) collective-permute-start(bf16[64,128]{1,0:T(8,128)(2,1)S(1)} %get-tuple-element.12), channel_id=1, source_target_pairs={{0,8},{8,0},{16,24},{24,16},{1,9},{9,1},{17,25},{25,17},{2,10},{10... | collective-permute-start | bytes 49160 | tf_op jit(solution)/shard_map/ppermute | solution.py:291

commit v11 on v10

--- a/solution.py
+++ b/solution.py
@@ -75,10 +75,14 @@
     samples_hbm,
     delay_hbm,
     tail_hbm,
+    table_hbm,
+    kernels_hbm,
     early_ref,
     moved,
     chosen,
     top_bin_ref,
+    table_ref,
+    kernels_ref,
     samples_ref,
     delay_ref,
     tail_ref,
@@ -132,6 +136,12 @@
     parity = jnp.where(own_shifts - 2.0 * jnp.floor(own_shifts * 0.5) == 0.0, one, -one)
 
     copies[2].wait()
+    copies = [
+        pltpu.make_async_copy(table_hbm, table_ref, arrived.at[3]),
+        pltpu.make_async_copy(kernels_hbm, kernels_ref, arrived.at[4]),
+    ]
+    for copy in copies:
+        copy.start()
     rows = moved.shape[0]
     turned[:STEP] = jnp.zeros((STEP, channels), jnp.float32)
     turned[STEP : STEP + block_len] = samples_ref[...].T.astype(jnp.float32)
@@ -174,6 +184,8 @@
     early = jnp.where(kept, early, 0.0) * (1.0 / math.sqrt(channels * chan_count))
     early_ref[...] = trial_blocks(early, chan_count).astype(jnp.bfloat16)
     top_bin_ref[...] = top_bin
+    for copy in copies:
+        copy.wait()
 
 
 def late_series(chan_count, scale, moved, chosen, top_bin_ref, late_ref, total):
@@ -259,22 +271,25 @@
     total_rows = block_len + STEP * (max(1, LANES // trials) - 1)
     total = pltpu.VMEM((total_rows, max(LANES, trials)), jnp.float32)
     group_rows = chan_count * ROWS
-    early, moved, chosen, top_bin = pl.pallas_call(
+    table = bin_table(block_len)
+    early, moved, chosen, top_bin, table_copy, kernels_copy = pl.pallas_call(
         functools.partial(partial_series, chan_count),
         out_shape=(
             jax.ShapeDtypeStruct((group_rows, LANES), jnp.bfloat16),
             jax.ShapeDtypeStruct((block_len + 2 * STEP, STEP * channels), jnp.bfloat16),
             jax.ShapeDtypeStruct((STEP * channels, block_len // STEP * trials), jnp.bfloat16),
             jax.ShapeDtypeStruct((trials, block_len), jnp.float32),
+            jax.ShapeDtypeStruct(table.shape, table.dtype),
+            jax.ShapeDtypeStruct(kernels.shape, kernels.dtype),
         ),
-        in_specs=[pl.BlockSpec(memory_space=pltpu.HBM)] * 3,
+        in_specs=[pl.BlockSpec(memory_space=pltpu.HBM)] * 5,
         scratch_shapes=[
             pltpu.VMEM((channels, block_len), jnp.bfloat16),
             pltpu.VMEM((chan_count, channels), jnp.int32),
             pltpu.VMEM((1, trials), jnp.int32),
             pltpu.VMEM((block_len + 3 * STEP, channels), jnp.float32),
             total,
-            pltpu.SemaphoreType.DMA((3,)),
+            pltpu.SemaphoreType.DMA((5,)),
         ],
         compiler_params=pltpu.CompilerParams(vmem_limit_bytes=40 * 1024 * 1024),
         name="partial_series",
@@ -285,6 +300,8 @@
                 filterbank,
                 chan_delay.reshape(chan_count, channels),
                 tail_len.reshape(1, trials),
+                table,
+                kernels,
             )
         )
     )
@@ -326,7 +343,7 @@
         ],
         compiler_params=pltpu.CompilerParams(vmem_limit_bytes=40 * 1024 * 1024),
         name="accel_search",
-    )(parts, bin_table(block_len), kernels)
+    )(parts, table_copy, kernels_copy)
     return power.reshape(accels, TRIAL_DEV, block_len // 2)
 
 

time: 15.8 us -> 15.9 us (level)
  no operation moved by 1% of the time
where the time goes in v11:
time: 15.9 us; the launch traced here: 15.7 us
  blocking collectives  11.3 us (71%)
  Pallas kernels  3.68 us (23%)
  starting transfers between devices  0.52 us (3%)
    all_to_all x1, blocking collectives, shards(): lax.all_to_all(parts, ('tm', 'chan'), 0, 0, axis_index_groups=group_order...  11.3 us
    pallas_call x1, Pallas kernels, shards(): pl.pallas_call(functools.partial(partial_series, chan_count), out_shape=(...  1.91 us
    pallas_call x1, Pallas kernels, shards(): pl.pallas_call(accel_search, out_shape=jax.ShapeDtypeStruct((accels * TRI...  1.09 us
    pallas_call x1, Pallas kernels, shards(): pl.pallas_call(functools.partial(late_series, chan_count, 1.0 / math.sqrt...  0.67 us
    ppermute x1, starting transfers between devices, shards(): lax.ppermute(early, 'tm', [(index, index ^ 1) for index in range(tm_count)])  0.52 us
  transfers between devices with their start and end apart: 1, of which 1 were waited for; matrix products, arithmetic and copies ran while one was open for 0% of the time, Pallas kernels for 4%

profile of v11, /device:TPU:0, one launch (start us, length us, event | category | flops | bytes accessed | tf_op | source)
XLA Modules:
  0.0 15.7 jit_solution(2126387279012798820)
XLA Ops:
  0.0 1.9 %partial_series.1 = (bf16[64,128]{1,0:T(8,128)(2,1)S(1)}, bf16[272,1024]{1,0:T(8,128)(2,1)S(1)}, bf16[1024,1024]{1,0:T(8,128)(2,1)S(1)}, f32[32,256]{1,0:T(8,128...) custom-call(bf16[128,256]{1,0:T(8,128)(2,1)} %samples_hbm.1, s32[8,128]{1,0:T(8,128)} %bitcast.7, ...), custom_call_target="tpu_custom_call" | custom-call | tf_op jit(solution)/shard_map/partial_series/pallas_call | solution.py:275
  1.9 0.5 %collective-permute-start = (bf16[64,128]{1,0:T(8,128)(2,1)S(1)}, bf16[64,128]{1,0:T(8,128)(2,1)S(1)}, u32[]{:S(2)}, u32[]{:S(2)}) collective-permute-start(bf16[64,128]{1,0:T(8,128)(2,1)S(1)} %get-tuple-element.14), channel_id=1, source_target_pairs={{0,8},{8,0},{16,24},{24,16},{1,9},{9,1},{17,25},{25,17},{2,10},{10... | collective-permute-start | bytes 49160 | tf_op jit(solution)/shard_map/ppermute | solution.py:308
  2.4 0.7 %late_series.1 = f32[64,128]{1,0:T(8,128)S(1)} custom-call(bf16[272,1024]{1,0:T(8,128)(2,1)S(1)} %get-tuple-element.11.moved, bf16[1024,1024]{1,0:T(8,128)(2,1)S(1)} %get-tuple-element.12.chosen, f32[32,256]{1,0:T(8,128)S(1)} %get-tuple-element.13.top_bin_ref), custom_call_target="tpu_custom_call" | custom-call | flops 536870912 | bytes 262144 | tf_op jit(solution)/shard_map/late_series/pallas_call | solution.py:309
  3.1 0.1 collective-permute-done
  3.3 11.3 %all_to_all.11 = bf16[16,8,128]{2,1,0:T(8,128)(2,1)S(1)} all-to-all(bf16[16,8,128]{2,1,0:T(8,128)(2,1)S(1)} %maximum_bitcast_fusion), channel_id=1, replica_groups={{15,8,9,10,11,12,13,14,23,16,17,18,19,20,21,22},{7,0,1,2,3,4,5,6,31,24,..., dimensions={0} | all-to-all | bytes 65536 | tf_op jit(solution)/shard_map/all_to_all | solution.py:329
  14.6 1.1 %accel_search.1 = bf16[128,128]{1,0:T(8,128)(2,1)} custom-call(bf16[128,128]{1,0:T(8,128)(2,1)S(1)} %bitcast.6, bf16[128,256]{1,0:T(8,128)(2,1)S(1)} %get-tuple-element.15.table_ref, bf16[2,32,256]{2,1,0:T(8,128)(2,1)S(1)} %get-tuple-element.16.kernels_ref), custom_call_target="tpu_custom_call" | custom-call | tf_op jit(solution)/shard_map/accel_search/pallas_call | solution.py:337
  (3 shorter events, 0.0 us)
Async XLA Ops:
  1.9 1.4 %collective-permute-start = (bf16[64,128]{1,0:T(8,128)(2,1)S(1)}, bf16[64,128]{1,0:T(8,128)(2,1)S(1)}, u32[]{:S(2)}, u32[]{:S(2)}) collective-permute-start(bf16[64,128]{1,0:T(8,128)(2,1)S(1)} %get-tuple-element.14), channel_id=1, source_target_pairs={{0,8},{8,0},{16,24},{24,16},{1,9},{9,1},{17,25},{25,17},{2,10},{10... | collective-permute-start | bytes 49160 | tf_op jit(solution)/shard_map/ppermute | solution.py:308

commit v12 on v10

--- a/solution.py
+++ b/solution.py
@@ -115,8 +115,8 @@
     def where_rest_is(value):
         return jnp.where(rests == jnp.array(value, jnp.bfloat16), one, zero)
 
-    def choose(first):
-        for fine in range(STEP):
+    def choose(first, fines=range(STEP)):
+        for fine in fines:
             for group in range(first, min(first + pair, groups)):
                 chosen[
                     fine * channels : (fine + 1) * channels, group * width : (group + 1) * width
@@ -125,8 +125,7 @@
     firsts = list(range(0, groups, pair))
     half = len(firsts) // 2
     firsts = firsts[half:][::-1] + firsts[:half]
-    for first in firsts[:1]:
-        choose(first)
+    choose(firsts[0], range(STEP // 2))
     own_shifts = shifts[:, :trials]
     whole = jnp.where(own_shifts == block_len, one, zero)
     parity = jnp.where(own_shifts - 2.0 * jnp.floor(own_shifts * 0.5) == 0.0, one, -one)
@@ -144,7 +143,9 @@
     end = block_len + step - STEP
     total[...] = jnp.zeros_like(total)
     for index, first in enumerate(firsts):
-        if index >= 1:
+        if index == 0:
+            choose(first, range(STEP // 2, STEP))
+        else:
             choose(first)
         last = min(first + pair, groups)
         sums = jnp.dot(

time: 15.8 us -> 15.9 us (level)
  no operation moved by 1% of the time
where the time goes in v12:
time: 15.9 us; the launch traced here: 15.7 us
  blocking collectives  11.3 us (71%)
  Pallas kernels  3.66 us (23%)
  starting transfers between devices  0.52 us (3%)
    all_to_all x1, blocking collectives, shards(): lax.all_to_all(parts, ('tm', 'chan'), 0, 0, axis_index_groups=group_order...  11.3 us
    pallas_call x1, Pallas kernels, shards(): pl.pallas_call(functools.partial(partial_series, chan_count), out_shape=(...  1.89 us
    pallas_call x1, Pallas kernels, shards(): pl.pallas_call(accel_search, out_shape=jax.ShapeDtypeStruct((accels * TRI...  1.09 us
    pallas_call x1, Pallas kernels, shards(): pl.pallas_call(functools.partial(late_series, chan_count, 1.0 / math.sqrt...  0.67 us
    ppermute x1, starting transfers between devices, shards(): lax.ppermute(early, 'tm', [(index, index ^ 1) for index in range(tm_count)])  0.52 us
  transfers between devices with their start and end apart: 1, of which 1 were waited for; matrix products, arithmetic and copies ran while one was open for 0% of the time, Pallas kernels for 4%

profile of v12, /device:TPU:0, one launch (start us, length us, event | category | flops | bytes accessed | tf_op | source)
XLA Modules:
  0.0 15.7 jit_solution(10606349235416875124)
XLA Ops:
  0.0 0.0 copy-start
  0.0 0.0 copy-start.1
  0.0 1.9 %partial_series.1 = (bf16[64,128]{1,0:T(8,128)(2,1)S(1)}, bf16[272,1024]{1,0:T(8,128)(2,1)S(1)}, bf16[1024,1024]{1,0:T(8,128)(2,1)S(1)}, f32[32,256]{1,0:T(8,128)S(1)}) custom-call(bf16[128,256]{1,0:T(8,128)(2,1)} %samples_hbm.1, s32[8,128]{1,0:T(8,128)} %bitcast.7, s32[1,32]{1,0:T(1,128)} %bitcast.8), custom_call_target="tpu_custom_call" | custom-call | tf_op jit(solution)/shard_map/partial_series/pallas_call | solution.py:263
  1.9 0.5 %collective-permute-start = (bf16[64,128]{1,0:T(8,128)(2,1)S(1)}, bf16[64,128]{1,0:T(8,128)(2,1)S(1)}, u32[]{:S(2)}, u32[]{:S(2)}) collective-permute-start(bf16[64,128]{1,0:T(8,128)(2,1)S(1)} %get-tuple-element.12), channel_id=1, source_target_pairs={{0,8},{8,0},{16,24},{24,16},{1,9},{9,1},{17,25},{25,17},{2,10},{10... | collective-permute-start | bytes 49160 | tf_op jit(solution)/shard_map/ppermute | solution.py:292
  2.4 0.7 %late_series.1 = f32[64,128]{1,0:T(8,128)S(1)} custom-call(bf16[272,1024]{1,0:T(8,128)(2,1)S(1)} %get-tuple-element.9.moved, bf16[1024,1024]{1,0:T(8,128)(2,1)S(1)} %get-tuple-element.10.chosen, f32[32,256]{1,0:T(8,128)S(1)} %get-tuple-element.11.top_bin_ref), custom_call_target="tpu_custom_call" | custom-call | flops 536870912 | bytes 262144 | tf_op jit(solution)/shard_map/late_series/pallas_call | solution.py:293
  3.1 0.1 collective-permute-done
  3.3 11.3 %all_to_all.11 = bf16[16,8,128]{2,1,0:T(8,128)(2,1)S(1)} all-to-all(bf16[16,8,128]{2,1,0:T(8,128)(2,1)S(1)} %maximum_bitcast_fusion), channel_id=1, replica_groups={{15,8,9,10,11,12,13,14,23,16,17,18,19,20,21,22},{7,0,1,2,3,4,5,6,31,24,..., dimensions={0} | all-to-all | bytes 65536 | tf_op jit(solution)/shard_map/all_to_all | solution.py:313
  14.6 0.0 copy-done
  14.6 0.0 copy-done.1
  14.6 1.1 %accel_search.1 = bf16[128,128]{1,0:T(8,128)(2,1)} custom-call(bf16[128,128]{1,0:T(8,128)(2,1)S(1)} %bitcast.6, bf16[128,256]{1,0:T(8,128)(2,1)S(1)} %copy-done, bf16[2,32,256]{2,1,0:T(8,128)(2,1)S(1)} %copy-done.1), custom_call_target="tpu_custom_call" | custom-call | tf_op jit(solution)/shard_map/accel_search/pallas_call | solution.py:321
  (3 shorter events, 0.0 us)
Async XLA Ops:
  0.0 14.6 %copy-start = (bf16[128,256]{1,0:T(8,128)(2,1)S(1)}, bf16[128,256]{1,0:T(8,128)(2,1)}, u32[]{:S(2)}) copy-start(bf16[128,256]{1,0:T(8,128)(2,1)} %constant.27.clone.table_ref) | copy-start | bytes 196612
  0.0 14.6 %copy-start.1 = (bf16[2,32,256]{2,1,0:T(8,128)(2,1)S(1)}, bf16[2,32,256]{2,1,0:T(8,128)(2,1)}, u32[]{:S(2)}) copy-start(bf16[2,32,256]{2,1,0:T(8,128)(2,1)} %kernels_ref.1) | copy-start | bytes 98308
  1.9 1.4 %collective-permute-start = (bf16[64,128]{1,0:T(8,128)(2,1)S(1)}, bf16[64,128]{1,0:T(8,128)(2,1)S(1)}, u32[]{:S(2)}, u32[]{:S(2)}) collective-permute-start(bf16[64,128]{1,0:T(8,128)(2,1)S(1)} %get-tuple-element.12), channel_id=1, source_target_pairs={{0,8},{8,0},{16,24},{24,16},{1,9},{9,1},{17,25},{25,17},{2,10},{10... | collective-permute-start | bytes 49160 | tf_op jit(solution)/shard_map/ppermute | solution.py:292
